TPU v7x, 32 devices: a whole 2x2x4 slice. The times are simulated.
32 devices in a mesh: groups: 2 (over y), ctx: 4 (over x, core), head: 4 (over z).
Axes of the slice: x: 2, y: 2, z: 4, core: 2. Of those that a mesh axis runs over, the one named last changes fastest.
Arguments:
- queries: bfloat16 [1536, 8, 5, 128], P(('groups', 'ctx'), 'head'), parts along dimension 0, may hold values from -6 to 6
- keys_values: bfloat16 [1536, 8, 2, 128], P(('groups', 'ctx'), 'head'), parts along dimension 0, may hold values from -6 to 6
- prior_state: bfloat16 [16, 8256, 128], P(('groups', 'head'), 'ctx'), parts along dimension 0, may hold values from -224 to 224
- counts: int32 [2], P('groups'), parts along dimension 0, may hold values from 384 to 1535
- continuation: int32 [64], P('groups'), parts along dimension 0, may hold values from 0 to 75967
- query_table: bfloat16 [75968, 8, 5, 128], P('ctx', 'head'), may hold values from -6 to 6
- pair_table: bfloat16 [75968, 8, 2, 128], P('ctx', 'head'), may hold values from -6 to 6
Outputs:
- readout: bfloat16 [1536, 8, 5, 128], P(('groups', 'ctx'), 'head'), parts along dimension 0
- decode_out: bfloat16 [64, 8, 5, 128], P(('groups', 'ctx'), 'head'), parts along dimension 0
- decode_state: float32 [16, 8256, 128], P(('groups', 'head'), 'ctx'), parts along dimension 0
There are 2 independent parts, one for each index of `groups`. A program takes and returns all parts, laid end to end along the dimension named above; an argument that names none is the same for every part. Nothing has to cross between parts.
All inputs are finite; a program needn't handle non-finite values.
Results may differ from a plain program's by a relative error of at most 0.0048.
The roundings to bfloat16 on the way count: a program that leaves them out, or rounds other values in their place, can miss the bound.
Values may be sent and summed in bfloat16 or wider, within the bound.
No kernel may reach another device: no remote copies, remote signals or barrier semaphores. Data moves between devices by JAX's collectives and lax.ppermute only.
A program may use at most 256 MiB of HBM per device.

v0:
```python
import functools

import jax
import jax.numpy as jnp
from jax import lax
from jax.experimental import pallas as pl
from jax.experimental.pallas import tpu as pltpu
from jax.sharding import PartitionSpec as P

ROOT_TWO = 2.0**0.5
AXIS = "ctx"
VMEM_LIMIT = 28 << 20
IN_VMEM = pl.BlockSpec(memory_space=pltpu.VMEM)
IN_SMEM = pl.BlockSpec(memory_space=pltpu.SMEM)
ANYWHERE = pl.BlockSpec(memory_space=pl.ANY)
IN_HBM = pl.BlockSpec(memory_space=pltpu.HBM)


def round_up(number, unit):
    return -(-number // unit) * unit


def params(limit=VMEM_LIMIT):
    return pltpu.CompilerParams(vmem_limit_bytes=limit)


def cost():
    return pl.CostEstimate(flops=1 << 10, bytes_accessed=1 << 10, transcendentals=0)


def swap(value, distance):
    count = lax.axis_size(AXIS)
    return lax.ppermute(value, AXIS, [(one, one ^ distance) for one in range(count)])


def distances(count):
    found = []
    step = count // 2
    while step:
        found.append(step)
        step //= 2
    return found


def gather_all(own, steps):
    held = {0: own}
    for step in steps:
        held.update({far ^ step: swap(shard, step) for far, shard in list(held.items())})
    return held


def pick_kernel(info_ref, ids_ref, qt_ref, pt_ref, *refs):
    rows, group = qt_ref.shape[:2]
    outs, sems = refs[:-1], refs[-1]
    steps = outs[0].shape[0]
    first = info_ref[0] * rows

    def targets(step):
        if len(outs) == 2:
            return outs[0].at[step], outs[1].at[step]
        return outs[0].at[step, :group], outs[0].at[step, group:]

    copies = []
    for step in range(steps):
        spot = jnp.clip(ids_ref[step] - first, 0, rows - 1)
        for at, (table, target) in enumerate(zip((qt_ref, pt_ref), targets(step))):
            copies.append(pltpu.make_async_copy(table.at[spot], target, sems.at[at, step]))
    for copy in copies:
        copy.start()
    for copy in copies:
        copy.wait()
    for step in range(steps):
        here = ids_ref[step] - first

        @pl.when(jnp.logical_or(here < 0, here >= rows))
        def _(step=step):
            for out in outs:
                out[step] = jnp.zeros(out.shape[1:], out.dtype)


def pick_rows(info, continuation, query_table, pair_table):
    steps = continuation.shape[0]
    parts = [query_table.shape[1:], pair_table.shape[1:]]
    joined = parts[0][1:] == parts[1][1:]
    if joined:
        parts = [(parts[0][0] + parts[1][0],) + parts[0][1:]]
    found = pl.pallas_call(
        pick_kernel,
        out_shape=[jax.ShapeDtypeStruct((steps,) + part, query_table.dtype) for part in parts],
        in_specs=[IN_SMEM, IN_SMEM, IN_HBM, IN_HBM],
        out_specs=[IN_VMEM] * len(parts),
        scratch_shapes=[pltpu.SemaphoreType.DMA((2, steps))],
        compiler_params=params(52 << 20),
        cost_estimate=cost(),
    )(info, continuation, query_table, pair_table)
    if joined:
        return found[0]
    spare = pair_table.shape[2] - query_table.shape[2]
    padded = jnp.pad(found[0], ((0, 0), (0, 0), (0, spare), (0, 0)))
    return jnp.concatenate([padded, found[1]], 1)


def feature_block(value, wide, block, first_block):
    width = value.shape[-1]
    shift = lax.rem(2 * width - first_block - block, width)
    scale = jnp.float32(ROOT_TWO)
    if block == 0:
        scale = jnp.where(first_block == 0, jnp.float32(1.0), scale)
    partner = pltpu.roll(value, shift, 1).astype(jnp.float32) * scale
    return (wide * partner).astype(jnp.bfloat16)


def feature_pairs(value, blocks, first_block):
    width = value.shape[-1]
    wide = value.astype(jnp.float32)
    for block in range(0, blocks, 2):
        parts = [
            feature_block(value, wide, at, first_block) for at in range(block, min(block + 2, blocks))
        ]
        yield block * width, jnp.concatenate(parts, 1) if len(parts) > 1 else parts[0]


class Span:
    def __init__(self, shards, count, shard_rows, width):
        self.shards, self.rows, self.width = shards, shard_rows, width
        self.total = shards * shard_rows
        self.blocks = max(
            -(-(self.total * at % width + self.total) // width) for at in range(count // shards)
        )
        self.shape = (self.blocks * width, width)
        self.aligned = shard_rows % 16 == 0

    def first_block(self, index):
        return lax.div(lax.div(index, self.shards) * self.total, self.width)

    def spot(self, index):
        at = lax.rem(lax.div(index, self.shards) * self.total, self.width)
        return at + lax.rem(index, self.shards) * self.rows

    def clear(self, ref):
        for edge in (slice(0, self.width), slice(self.shape[0] - self.width, self.shape[0])):
            ref[edge] = jnp.zeros((self.width, self.width), ref.dtype)

    def place(self, source, ref, index, first, sem):
        spot = pl.multiple_of(self.spot(index) + first, 16)
        return pltpu.make_async_copy(source, ref.at[pl.ds(spot, source.shape[0])], sem)

    def room(self, held, me):
        room = jnp.zeros(self.shape, held[0][2].dtype)
        for slot, first, rows in held:
            room = lax.dynamic_update_slice_in_dim(room, rows, self.spot(me ^ slot) + first, 0)
        return room


class States:
    def __init__(self, span, lists):
        self.span, self.arrays, self.plan = span, [], []
        for pieces in lists:
            entry = []
            for array, head, slot, first in pieces:
                if not any(array is one for one in self.arrays):
                    self.arrays.append(array)
                place = [array is one for one in self.arrays].index(True)
                entry.append((place, head, slot, first))
            self.plan.append(entry)

    def scratch(self):
        copies = sum(len(entry) for entry in self.plan)
        return [pltpu.VMEM(self.span.shape, jnp.bfloat16)] * len(self.plan) + [
            pltpu.SemaphoreType.DMA((copies,))
        ]

    def bring(self, refs, scratch, info_ref):
        buffers, sems = scratch[:-1], scratch[-1]
        copies = []
        for buffer, entry in zip(buffers, self.plan):
            if self.span.aligned:
                self.span.clear(buffer)
            for place, head, slot, first in entry:
                source = refs[place] if head is None else refs[place].at[head]
                sem = sems.at[len(copies)]
                if self.span.aligned:
                    copies.append(self.span.place(source, buffer, info_ref[slot], first, sem))
                else:
                    copies.append(pltpu.make_async_copy(source, buffer, sem))
        for copy in copies:
            copy.start()
        return copies


def carried(value, state_ref, span, first_block, out_ref, fresh):
    for start, part in feature_pairs(value, span.blocks, first_block):
        added = jnp.dot(
            part, state_ref[start : start + part.shape[1]], preferred_element_type=jnp.float32
        )
        if fresh and start == 0:
            out_ref[...] = added
        else:
            out_ref[...] += added


def by_head(value):
    return jnp.swapaxes(value, 0, 1)


def near_kernel(span, states, info_ref, q_ref, *refs):
    ins = refs[: len(states.arrays)]
    sum_ref = refs[len(states.arrays)]
    scratch = refs[len(states.arrays) + 1 :]
    copies = states.bring(ins, scratch, info_ref)
    query = by_head(q_ref[...])
    first_block = span.first_block(info_ref[0])
    for copy in copies:
        copy.wait()
    for head in range(query.shape[0]):
        carried(query[head], scratch[head], span, first_block, sum_ref.at[head], True)


def near_sums(info, query, span, states):
    rows, heads, width = query.shape
    return pl.pallas_call(
        functools.partial(near_kernel, span, states),
        out_shape=jax.ShapeDtypeStruct((heads, rows, width), jnp.float32),
        in_specs=[IN_SMEM, IN_VMEM] + [ANYWHERE] * len(states.arrays),
        out_specs=IN_VMEM,
        scratch_shapes=states.scratch(),
        compiler_params=params(),
        cost_estimate=cost(),
    )(info, query, *states.arrays)


def squared_sum(query, keys, values, scale, bound):
    scores = lax.dot_general(
        query, keys, (((1,), (1,)), ((), ())), preferred_element_type=jnp.float32
    )
    row = lax.broadcasted_iota(jnp.int32, scores.shape, 0)
    weights = jnp.where(bound <= row, scores * scores * scale, 0.0).astype(jnp.bfloat16)
    return jnp.dot(weights, values, preferred_element_type=jnp.float32)


def columns(count):
    return lax.broadcasted_iota(jnp.int32, (1, count), 1)


def step_parts(final_ref, heads, step_rows, steps):
    queries = by_head(final_ref[:step_rows])
    pairs = [
        by_head(final_ref[step_rows + head * steps : step_rows + (head + 1) * steps])
        for head in range(heads)
    ]
    return queries, pairs


def keys_kernel(
    slots, group, steps, span, info_ref, q_ref, mine_ref, theirs_ref, prior_ref, near_ref, *refs
):
    kv_refs = refs[:slots]
    sum_ref, step_ref, f_ref, state_ref, rows_ref = refs[slots:]
    f_ref[...] = mine_ref[...] + theirs_ref[...]
    rows, heads, width = q_ref.shape
    step_rows = step_ref.shape[1]
    me = info_ref[0]
    query = by_head(q_ref[...])
    step_query, step_pairs = step_parts(f_ref, heads, step_rows, steps)
    first_block = span.first_block(me)
    keys = kv_refs[0].shape[0]
    unit = 1.0 / width
    for head in range(heads):
        pairs = [by_head(kv_ref[:, head]) for kv_ref in kv_refs]
        total = near_ref[head] * unit
        steps_total = None
        for start in range(0, slots, 4):
            part = pairs[start : start + 4]
            column = columns(len(part) * keys)
            scale = jnp.zeros(column.shape, jnp.float32)
            for at in range(len(part)):
                used = jnp.logical_or(info_ref[start + at] < me, start + at == 0)
                factor = jnp.where(used, jnp.float32(unit), jnp.float32(0.0))
                scale = jnp.where(column >= at * keys, factor, scale)
            bound = jnp.where(column < keys, column * group, 0) if start == 0 else column * 0
            part_keys = jnp.concatenate([pair[0] for pair in part], 0)
            part_values = jnp.concatenate([pair[1] for pair in part], 0)
            total = total + squared_sum(query[head], part_keys, part_values, scale, bound)
            full = jnp.full(column.shape, unit, jnp.float32)
            added = squared_sum(step_query[head], part_keys, part_values, full, column * 0)
            steps_total = added if steps_total is None else steps_total + added
        sum_ref[head] = total
        key, value = step_pairs[head][0], step_pairs[head][1]
        column = columns(steps)
        full = jnp.full(column.shape, unit, jnp.float32)
        step_ref[head] = steps_total + squared_sum(
            step_query[head], key, value, full, (column - info_ref[slots]) * group
        )
        all_keys = jnp.concatenate([pair[0] for pair in pairs] + [key], 0)
        all_values = jnp.concatenate([pair[1] for pair in pairs] + [value], 0)
        turned = all_values.astype(jnp.float32).T.astype(jnp.bfloat16)
        for start, part in feature_pairs(all_keys, span.blocks, first_block):
            added = jnp.dot(turned, part, preferred_element_type=jnp.float32).T
            if span.aligned:
                rows_ref[start : start + part.shape[1]] = added
            else:
                state_ref[head, start : start + part.shape[1]] = added
        if span.aligned:
            spot = pl.multiple_of(span.spot(me), 16)
            state_ref[head] = prior_ref[head].astype(jnp.float32) + rows_ref[pl.ds(spot, span.rows)]


def key_sums(info, query, mine, theirs, prior, near, pairs, step_rows, steps, group, span):
    rows, heads, width = query.shape
    slots = len(pairs)
    state_shape = prior.shape if span.aligned else (heads,) + span.shape
    return pl.pallas_call(
        functools.partial(keys_kernel, slots, group, steps, span),
        out_shape=[
            jax.ShapeDtypeStruct((heads, rows, width), jnp.float32),
            jax.ShapeDtypeStruct((heads, step_rows, width), jnp.float32),
            jax.ShapeDtypeStruct(mine.shape, mine.dtype),
            jax.ShapeDtypeStruct(state_shape, jnp.float32),
        ],
        in_specs=[IN_SMEM] + [IN_VMEM] * (5 + slots),
        out_specs=[IN_VMEM] * 4,
        scratch_shapes=[pltpu.VMEM(span.shape, jnp.float32)],
        compiler_params=params(),
        cost_estimate=cost(),
    )(info, query, mine, theirs, prior, near, *[pairs[slot] for slot in range(slots)])


def far_kernel(head, group, count, tokens, span, states, outputs, info_ref, q_ref, f_ref, *refs):
    ins, refs = refs[: len(states.arrays)], refs[len(states.arrays) :]
    sum_ref, step_ref, refs = refs[0], refs[1], refs[2:]
    taken = 3 if head else 0
    earlier, refs = refs[:taken], refs[taken:]
    results, refs = refs[:outputs], refs[outputs:]
    total_ref, scratch = refs[0], refs[1 : 2 + len(states.plan)]
    rows, heads, width = q_ref.shape
    step_rows = step_ref.shape[1]
    copies = states.bring(ins, scratch, info_ref)
    query = by_head(q_ref[...])
    step_query = by_head(f_ref[:step_rows])
    first_block = span.first_block(info_ref[0])
    far_block = span.first_block(info_ref[count // 2])
    for copy in copies:
        copy.wait()
    both = jnp.concatenate([query[head], step_query[head]], 0)
    carried(both, scratch[len(states.plan) - 1], span, far_block, total_ref, True)
    if head:
        near_ref = earlier[2]
    else:
        near_ref = results[2] if heads > 1 else refs[-1]
        for one in range(heads):
            carried(step_query[one], scratch[one], span, first_block, near_ref.at[one], True)
    start = info_ref[count + 1] + 1
    found = []
    for own, total, first in (
        (sum_ref[head], total_ref[:rows], start + info_ref[0] * tokens),
        (
            step_ref[head],
            total_ref[rows:] + near_ref[head],
            start + count * tokens + info_ref[count],
        ),
    ):
        row = lax.broadcasted_iota(jnp.int32, own.shape, 0).astype(jnp.float32)
        token = jnp.floor((row + 0.5) * (1.0 / group))
        position = token + first.astype(jnp.float32)
        found.append((total * (1.0 / width) + own) / jnp.sqrt(position))
    for at in range(2):
        if head < heads - 1:
            done = [earlier[at][one] for one in range(head)] + [found[at]]
            for one, value in enumerate(done):
                results[at][one] = value
        else:
            done = [earlier[at][one] for one in range(head)] + [found[at]]
            results[at][...] = jnp.stack(done, 1).astype(jnp.bfloat16)


def far_sums(head, info, query, final, sums, step_sums, earlier, group, count, span, states):
    rows, heads, width = query.shape
    step_rows = step_sums.shape[1]
    held = [pltpu.VMEM((rows + step_rows, width), jnp.float32)]
    near = jax.ShapeDtypeStruct((heads, step_rows, width), jnp.float32)
    if head == heads - 1:
        shapes = [
            jax.ShapeDtypeStruct((rows, heads, width), jnp.bfloat16),
            jax.ShapeDtypeStruct((step_rows, heads, width), jnp.bfloat16),
        ]
    else:
        shapes = [
            jax.ShapeDtypeStruct((head + 1, rows, width), jnp.float32),
            jax.ShapeDtypeStruct((head + 1, step_rows, width), jnp.float32),
        ] + ([near] if head == 0 else [])
    spare = [pltpu.VMEM(near.shape, near.dtype)] if heads == 1 else []
    return pl.pallas_call(
        functools.partial(
            far_kernel, head, group, count, rows // group, span, states, len(shapes)
        ),
        out_shape=shapes,
        in_specs=[IN_SMEM]
        + [IN_VMEM] * 2
        + [ANYWHERE] * len(states.arrays)
        + [IN_VMEM] * (2 + len(earlier)),
        out_specs=[IN_VMEM] * len(shapes),
        scratch_shapes=held + states.scratch() + spare,
        compiler_params=params(),
        cost_estimate=cost(),
    )(info, query, final, *states.arrays, sums, step_sums, *earlier)


def on_device(queries, keys_values, prior_state, counts, continuation, query_table, pair_table):
    tokens, heads, group, width = queries.shape
    count = lax.axis_size(AXIS)
    me = lax.axis_index(AXIS)
    shard_rows = prior_state.shape[1]
    steps = continuation.shape[0]
    own_steps = steps // count
    step_rows = own_steps * group
    slots = range(count)
    far, nearer = distances(count)[0], distances(count)[1:]
    info = jnp.stack([me ^ slot for slot in slots] + [me * own_steps, counts[0]]).astype(jnp.int32)

    pairs = gather_all(keys_values, [far] + nearer)
    near_prior = gather_all(prior_state, nearer)

    half = shard_rows // 2
    half = round_up(half, 16) if shard_rows % 16 == 0 else half
    cuts = [(0, half), (half, shard_rows)]
    parts = [(head, first, prior_state[head, first:stop]) for head in range(heads) for first, stop in cuts]
    opening, continuation = lax.optimization_barrier((parts[0][2], continuation))
    parts[0] = (0, 0, opening)

    picked = pick_rows(
        info, continuation, jnp.transpose(query_table, (0, 2, 1, 3)), pair_table
    )
    for step in reversed(nearer):
        picked = picked + swap(picked, step)

    def share(index):
        mine = lax.dynamic_slice_in_dim(picked[:, :group], index * own_steps, own_steps, 0)
        pair = jnp.transpose(picked[:, group:], (1, 0, 2, 3))
        return jnp.concatenate(
            [mine.reshape(step_rows, 2, width), pair.reshape(heads * steps, 2, width)], 0
        )

    outgoing = share(me ^ far)
    mine, theirs = share(me), swap(outgoing, far)
    arrived = [swap(opening, far)]
    for head, first, rows in parts[1:]:
        rows, _ = lax.optimization_barrier((rows, outgoing))
        arrived.append(swap(rows, far))

    def passed_on(at, after):
        head, first, _ = parts[at]
        rows, _ = lax.optimization_barrier((arrived[at], after))
        return [(slot ^ far, first, part) for slot, part in sorted(gather_all(rows, nearer).items())]

    query = jnp.transpose(queries, (0, 2, 1, 3)).reshape(tokens * group, heads, width)
    span = Span(far, count, shard_rows, width)
    own_span = Span(1, count, shard_rows, width)

    def pieces(held, head):
        if span.aligned:
            return [(rows, None if rows.ndim == 2 else head, slot, first) for slot, first, rows in held]
        held = [(slot, first, rows if rows.ndim == 2 else rows[head]) for slot, first, rows in held]
        return [(span.room(held, me), None, 0, 0)]

    near_held = [(slot, 0, rows) for slot, rows in sorted(near_prior.items())]
    near_pieces = [pieces(near_held, head) for head in range(heads)]
    near = near_sums(info, query, span, States(span, near_pieces))
    held = [passed_on(0, near)]
    sums, step_sums, final, decode_state = key_sums(
        info, query, mine, theirs, prior_state, near, pairs, step_rows, steps, group, own_span
    )
    held.append(passed_on(1, sums))
    if not own_span.aligned:
        added = lax.dynamic_slice_in_dim(decode_state, own_span.spot(me), shard_rows, 1)
        decode_state = prior_state.astype(jnp.float32) + added
    earlier = []
    for head in range(heads):
        far_pieces = pieces(held[2 * head] + held[2 * head + 1], head)
        states = States(span, (near_pieces if head == 0 else []) + [far_pieces])
        found = far_sums(
            head, info, query, final, sums, step_sums, earlier, group, count, span, states
        )
        earlier = list(found[:2]) + (earlier[2:] if head else list(found[2:]))
        if head < heads - 1:
            held += [passed_on(2 * head + 2, found[0]), passed_on(2 * head + 3, found[0])]
    readout, decode_out = earlier[:2]
    readout = jnp.transpose(readout.reshape(tokens, group, heads, width), (0, 2, 1, 3))
    decode_out = jnp.transpose(decode_out.reshape(own_steps, group, heads, width), (0, 2, 1, 3))
    return (readout, decode_out, decode_state)


def solution(mesh):
    in_specs = (
        P(("groups", "ctx"), "head", None, None),
        P(("groups", "ctx"), "head", None, None),
        P(("groups", "head"), "ctx", None),
        P("groups"),
        P("groups"),
        P("ctx", "head", None, None),
        P("ctx", "head", None, None),
    )
    out_specs = (
        P(("groups", "ctx"), "head", None, None),
        P(("groups", "ctx"), "head", None, None),
        P(("groups", "head"), "ctx", None),
    )
    return jax.shard_map(
        on_device, mesh=mesh, in_specs=in_specs, out_specs=out_specs, check_vma=False
    )
```

profile of v0, /device:TPU:0, one launch (start us, length us, event | category | flops | bytes accessed | tf_op | source)
XLA Modules:
  0.0 51.5 jit_solution(17215879033590547076)
XLA Ops:
  0.6 0.0 copy-start.3
  0.6 0.5 %collective-permute-start.2 = (bf16[2,2064,128]{2,1,0:T(8,128)(2,1)}, bf16[2,2064,128]{2,1,0:T(8,128)(2,1)S(1)}, u32[]{:S(2)}, u32[]{:S(2)}) collective-permute-start(bf16[2,2064,128]{2,1,0:T(8,128)(2,1)} %refs_0_.5), channel_id=1, source_target_pairs={{0,4},{4,0},{8,12},{12,8},{1,5},{5,1},{9,13},{13,9},{2,6},{6,2},{1... | collective-permute-start | bytes 3170312 | tf_op jit(solution)/shard_map/ppermute | solution.py:33
  1.2 1.9 %slice_bitcast_fusion = (bf16[1040,128]{1,0:T(8,128)(2,1)}, bf16[1040,128]{1,0:T(8,128)(2,1)}) fusion(bf16[2,2064,128]{2,1,0:T(8,128)(2,1)} %refs_0_.5), kind=kLoop, calls=%fused_computation | loop fusion | bytes 1064960 | tf_op jit(solution)/shard_map/squeeze | solution.py:426
  3.7 0.1 stack.23.info_ref
  3.8 0.0 copy-done.3
  3.8 0.0 copy-start
  3.8 2.9 %shard_map.94 = bf16[32,7,2,128]{3,2,1,0:T(2,128)(2,1)S(1)} custom-call(s32[6]{0:T(128)S(1)} %stack.23.info_ref, s32[32]{0:T(128)S(1)} %copy-done.3, bf16[18992,5,2,128]{3,2,1,0:T(2,128)(2,1)} %bitcast.32, bf16[18992,2,2,128]{3,2,1,0:T(2,128)(2,1)} %pt_ref.1), custom_call_target="tpu_custom_call" | custom-call | flops 1024 | bytes 1024 | tf_op jit(solution)/shard_map/pallas_call | solution.py:87
  6.7 0.0 copy-start.1
  6.7 0.1 collective-permute-start
  6.8 0.0 copy-done.2
  6.8 2.8 %collective-permute-start.4 = (bf16[192,2,2,128]{3,2,1,0:T(2,128)(2,1)S(1)}, bf16[192,2,2,128]{3,2,1,0:T(2,128)(2,1)S(1)}, u32[]{:S(2)}, u32[]{:S(2)}) collective-permute-start(bf16[192,2,2,128]{3,2,1,0:T(2,128)(2,1)S(1)} %copy-done.2), channel_id=1, source_target_pairs={{0,8},{4,12},{8,0},{12,4},{1,9},{5,13},{9,1},{13,5},{2,10},{6,14},... | collective-permute-start | bytes 589832 | tf_op jit(solution)/shard_map/ppermute | solution.py:33
  9.6 0.0 collective-permute-start.7
  9.7 0.0 copy-done
  9.7 0.8 %slice_bitcast_fusion.2 = (bf16[1024,128]{1,0:T(8,128)(2,1)}, bf16[1024,128]{1,0:T(8,128)(2,1)}) fusion(bf16[2,2064,128]{2,1,0:T(8,128)(2,1)S(1)} %copy-done), kind=kLoop, calls=%fused_computation.2 | loop fusion | bytes 1048576 | tf_op jit(solution)/shard_map/squeeze | solution.py:426
  10.5 0.0 collective-permute-done
  10.5 0.1 add.9
  10.6 0.1 slice.26
  10.8 0.1 pad_maximum_fusion.1
  10.9 2.1 %collective-permute-start.9 = (bf16[1024,128]{1,0:T(8,128)(2,1)}, bf16[1024,128]{1,0:T(8,128)(2,1)S(1)}, u32[]{:S(2)}, u32[]{:S(2)}) collective-permute-start(bf16[1024,128]{1,0:T(8,128)(2,1)} %get-tuple-element.26), channel_id=1, source_target_pairs={{0,8},{4,12},{8,0},{12,4},{1,9},{5,13},{9,1},{13,5},{2,10},{6,14},... | collective-permute-start | bytes 786440 | tf_op jit(solution)/shard_map/ppermute | solution.py:33
  13.0 0.0 collective-permute-start.3
  13.0 2.3 %collective-permute-done.4.refs_2_ = bf16[192,2,2,128]{3,2,1,0:T(2,128)(2,1)S(1)} collective-permute-done((bf16[192,2,2,128]{3,2,1,0:T(2,128)(2,1)S(1)}, bf16[192,2,2,128]{3,2,1,0:T(2,128)(2,1)S(1)}, u32[]{:S(2)}, u32[]{:S(2)}) %collective-permute-start.4) | collective-permute-done | bytes 196640 | tf_op jit(solution)/shard_map/ppermute | solution.py:33
  15.3 0.0 collective-permute-start.5
  15.3 0.0 collective-permute-done.2.refs_1_
  15.3 2.1 %collective-permute-start.1 = (bf16[104,2,128]{2,1,0:T(2,128)(2,1)S(1)}, bf16[104,2,128]{2,1,0:T(2,128)(2,1)S(1)}, u32[]{:S(2)}, u32[]{:S(2)}) collective-permute-start(bf16[104,2,128]{2,1,0:T(2,128)(2,1)S(1)} %get-tuple-element.45), channel_id=1, source_target_pairs={{0,8},{4,12},{8,0},{12,4},{1,9},{5,13},{9,1},{13,5},{2,10},{6,14},... | collective-permute-start | bytes 159752 | tf_op jit(solution)/shard_map/ppermute | solution.py:33
  17.4 0.0 copy-done.1
  17.4 5.2 %shard_map.95.near_ref = f32[2,960,128]{2,1,0:T(8,128)S(1)} custom-call(s32[6]{0:T(128)S(1)} %stack.23.info_ref, bf16[960,2,128]{2,1,0:T(2,128)(2,1)S(1)} %bitcast.28, bf16[2,2064,128]{2,1,0:T(8,128)(2,1)S(1)} %copy-done, bf16[2,2064,128]{2,1,0:T(8,128)(2,1)S(1)} %collective-permute-done.2.refs_1_), custom_call_target="tpu_custom_call" | custom-call | flops 1024 | bytes 1024 | tf_op jit(solution)/shard_map/pallas_call | solution.py:221
  22.6 0.0 collective-permute-done.7.refs_2_
  22.7 0.3 collective-permute-start.8
  22.9 4.3 %collective-permute-done.1.theirs_ref = bf16[104,2,128]{2,1,0:T(2,128)(2,1)S(1)} collective-permute-done((bf16[104,2,128]{2,1,0:T(2,128)(2,1)S(1)}, bf16[104,2,128]{2,1,0:T(2,128)(2,1)S(1)}, u32[]{:S(2)}, u32[]{:S(2)}) %collective-permute-start.1) | collective-permute-done | bytes 53280 | tf_op jit(solution)/shard_map/ppermute | solution.py:33
  27.2 0.0 copy-done.4
  27.2 1.7 %collective-permute-start.6 = (bf16[1040,128]{1,0:T(8,128)(2,1)S(1)}, bf16[1040,128]{1,0:T(8,128)(2,1)S(1)}, u32[]{:S(2)}, u32[]{:S(2)}) collective-permute-start(bf16[1040,128]{1,0:T(8,128)(2,1)S(1)} %copy-done.4), channel_id=1, source_target_pairs={{0,8},{4,12},{8,0},{12,4},{1,9},{5,13},{9,1},{13,5},{2,10},{6,14},... | collective-permute-start | bytes 798728 | tf_op jit(solution)/shard_map/ppermute | solution.py:33
  29.0 0.0 collective-permute-done.3.refs_1_
  29.0 0.0 collective-permute-done.5.refs_3_
  29.0 7.1 %shard_map.96 = (f32[2,960,128]{2,1,0:T(8,128)S(1)}, f32[2,40,128]{2,1,0:T(8,128)S(1)}, bf16[104,2,128]{2,1,0:T(2,128)(2,1)S(1)}, f32[2,2064,128]{2,1,0:T(8,128)}) custom-call(s32[6]{0:T(128)S(1)} %stack.23.info_ref, bf16[960,2,128]{2,1,0:T(2,128)(2,1)S(1)} %bitcast.29, bf16[104,2,128]{2,1,0:T(2,128)(2,1)S(1)} %get-tuple-element.46.mine_ref, ...), custom_call_target="tpu_custom_call" | custom-call | flops 1024 | bytes 1024 | tf_op jit(solution)/shard_map/pallas_call | solution.py:312
  36.1 0.0 collective-permute-done.9.refs_4_
  36.1 0.0 collective-permute-start.10
  36.1 0.0 copy-done.5
  36.1 0.3 collective-permute-start.12
  36.5 1.2 %collective-permute-done.10.refs_5_ = bf16[1024,128]{1,0:T(8,128)(2,1)S(1)} collective-permute-done((bf16[1024,128]{1,0:T(8,128)(2,1)S(1)}, bf16[1024,128]{1,0:T(8,128)(2,1)S(1)}, u32[]{:S(2)}, u32[]{:S(2)}) %collective-permute-start.10) | collective-permute-done | bytes 262176 | tf_op jit(solution)/shard_map/ppermute | solution.py:33
  37.7 0.0 collective-permute-done.8.refs_3_
  37.7 4.5 %shard_map.97 = (f32[1,960,128]{2,1,0:T(8,128)S(1)}, f32[1,40,128]{2,1,0:T(8,128)S(1)}, f32[2,40,128]{2,1,0:T(8,128)S(1)}) custom-call(s32[6]{0:T(128)S(1)} %stack.23.info_ref, bf16[960,2,128]{2,1,0:T(2,128)(2,1)S(1)} %bitcast.30, bf16[104,2,128]{2,1,0:T(2,128)(2,1)S(1)} %get-tuple-element.22.f_ref, bf16[2,2064,128]{2,1,0:T(8,128)(2,1)S(1)} %copy-done, ...), custom_call_target="tpu_custom_call" | custom-call | flops 1024 | bytes 1024 | tf_op jit(solution)/shard_map/pallas_call | solution.py:392
  42.2 0.0 collective-permute-done.6.refs_0_
  42.2 0.2 collective-permute-start.11
  42.4 2.5 %collective-permute-done.12.refs_2_ = bf16[1024,128]{1,0:T(8,128)(2,1)S(1)} collective-permute-done((bf16[1024,128]{1,0:T(8,128)(2,1)S(1)}, bf16[1024,128]{1,0:T(8,128)(2,1)S(1)}, u32[]{:S(2)}, u32[]{:S(2)}) %collective-permute-start.12) | collective-permute-done | bytes 262176 | tf_op jit(solution)/shard_map/ppermute | solution.py:33
  44.8 0.0 collective-permute-start.13
  44.8 1.5 %collective-permute-done.13.refs_3_ = bf16[1024,128]{1,0:T(8,128)(2,1)S(1)} collective-permute-done((bf16[1024,128]{1,0:T(8,128)(2,1)S(1)}, bf16[1024,128]{1,0:T(8,128)(2,1)S(1)}, u32[]{:S(2)}, u32[]{:S(2)}) %collective-permute-start.13) | collective-permute-done | bytes 262176 | tf_op jit(solution)/shard_map/ppermute | solution.py:33
  46.4 0.0 collective-permute-done.11.refs_1_
  46.4 4.9 %shard_map.98 = (bf16[960,2,128]{2,1,0:T(2,128)(2,1)}, bf16[40,2,128]{2,1,0:T(2,128)(2,1)}) custom-call(s32[6]{0:T(128)S(1)} %stack.23.info_ref, bf16[960,2,128]{2,1,0:T(2,128)(2,1)S(1)} %bitcast.31, bf16[104,2,128]{2,1,0:T(2,128)(2,1)S(1)} %get-tuple-element.22.f_ref, bf16[1040,128]{1,0:T(8,128)(2,1)S(1)} %collective-permute-done.6.refs_0_, ...), custom_call_target="tpu_custom_call" | custom-call | flops 1024 | bytes 1024 | tf_op jit(solution)/shard_map/pallas_call | solution.py:392
  (6 shorter events, 0.1 us)
Async XLA Ops:
  0.6 3.1 %copy-start.3 = (s32[32]{0:T(128)S(1)}, s32[32]{0:T(128)}, u32[]{:S(2)}) copy-start(s32[32]{0:T(128)} %ids_ref) | copy-start | bytes 388
  0.6 14.7 %collective-permute-start.2 = (bf16[2,2064,128]{2,1,0:T(8,128)(2,1)}, bf16[2,2064,128]{2,1,0:T(8,128)(2,1)S(1)}, u32[]{:S(2)}, u32[]{:S(2)}) collective-permute-start(bf16[2,2064,128]{2,1,0:T(8,128)(2,1)} %refs_0_.5), channel_id=1, source_target_pairs={{0,4},{4,0},{8,12},{12,8},{1,5},{5,1},{9,13},{13,9},{2,6},{6,2},{1... | collective-permute-start | bytes 3170312 | tf_op jit(solution)/shard_map/ppermute | solution.py:33
  3.8 3.0 %copy-start.2 = (bf16[192,2,2,128]{3,2,1,0:T(2,128)(2,1)S(1)}, bf16[192,2,2,128]{3,2,1,0:T(2,128)(2,1)}, u32[]{:S(2)}) copy-start(bf16[192,2,2,128]{3,2,1,0:T(2,128)(2,1)} %refs_0_.4) | copy-start | bytes 589828
  3.8 5.9 %copy-start = (bf16[2,2064,128]{2,1,0:T(8,128)(2,1)S(1)}, bf16[2,2064,128]{2,1,0:T(8,128)(2,1)}, u32[]{:S(2)}) copy-start(bf16[2,2064,128]{2,1,0:T(8,128)(2,1)} %refs_0_.5) | copy-start | bytes 3170308
  6.7 10.7 %copy-start.1 = (bf16[192,2,5,128]{3,1,2,0:T(2,128)(2,1)S(1)}, bf16[192,2,5,128]{3,1,2,0:T(2,128)(2,1)}, u32[]{:S(2)}) copy-start(bf16[192,2,5,128]{3,1,2,0:T(2,128)(2,1)} %param.7) | copy-start | bytes 1474564
  6.7 3.8 %collective-permute-start = (bf16[32,7,2,128]{3,2,1,0:T(2,128)(2,1)S(1)}, bf16[32,7,2,128]{3,2,1,0:T(2,128)(2,1)S(1)}, u32[]{:S(2)}, u32[]{:S(2)}) collective-permute-start(bf16[32,7,2,128]{3,2,1,0:T(2,128)(2,1)S(1)} %shard_map.94), channel_id=1, source_target_pairs={{0,4},{4,0},{8,12},{12,8},{1,5},{5,1},{9,13},{13,9},{2,6},{6,2},{1... | collective-permute-start | bytes 344072 | tf_op jit(solution)/shard_map/ppermute | solution.py:33
  6.8 8.5 %collective-permute-start.4 = (bf16[192,2,2,128]{3,2,1,0:T(2,128)(2,1)S(1)}, bf16[192,2,2,128]{3,2,1,0:T(2,128)(2,1)S(1)}, u32[]{:S(2)}, u32[]{:S(2)}) collective-permute-start(bf16[192,2,2,128]{3,2,1,0:T(2,128)(2,1)S(1)} %copy-done.2), channel_id=1, source_target_pairs={{0,8},{4,12},{8,0},{12,4},{1,9},{5,13},{9,1},{13,5},{2,10},{6,14},... | collective-permute-start | bytes 589832 | tf_op jit(solution)/shard_map/ppermute | solution.py:33
  9.6 13.0 %collective-permute-start.7 = (bf16[1040,128]{1,0:T(8,128)(2,1)}, bf16[1040,128]{1,0:T(8,128)(2,1)S(1)}, u32[]{:S(2)}, u32[]{:S(2)}) collective-permute-start(bf16[1040,128]{1,0:T(8,128)(2,1)} %get-tuple-element.24), channel_id=1, source_target_pairs={{0,8},{4,12},{8,0},{12,4},{1,9},{5,13},{9,1},{13,5},{2,10},{6,14},... | collective-permute-start | bytes 798728 | tf_op jit(solution)/shard_map/ppermute | solution.py:33
  10.9 25.2 %collective-permute-start.9 = (bf16[1024,128]{1,0:T(8,128)(2,1)}, bf16[1024,128]{1,0:T(8,128)(2,1)S(1)}, u32[]{:S(2)}, u32[]{:S(2)}) collective-permute-start(bf16[1024,128]{1,0:T(8,128)(2,1)} %get-tuple-element.26), channel_id=1, source_target_pairs={{0,8},{4,12},{8,0},{12,4},{1,9},{5,13},{9,1},{13,5},{2,10},{6,14},... | collective-permute-start | bytes 786440 | tf_op jit(solution)/shard_map/ppermute | solution.py:33
  13.0 16.0 %collective-permute-start.3 = (bf16[192,2,2,128]{3,2,1,0:T(2,128)(2,1)S(1)}, bf16[192,2,2,128]{3,2,1,0:T(2,128)(2,1)S(1)}, u32[]{:S(2)}, u32[]{:S(2)}) collective-permute-start(bf16[192,2,2,128]{3,2,1,0:T(2,128)(2,1)S(1)} %copy-done.2), channel_id=1, source_target_pairs={{0,4},{4,0},{8,12},{12,8},{1,5},{5,1},{9,13},{13,9},{2,6},{6,2},{1... | collective-permute-start | bytes 589832 | tf_op jit(solution)/shard_map/ppermute | solution.py:33
  15.3 13.7 %collective-permute-start.5 = (bf16[192,2,2,128]{3,2,1,0:T(2,128)(2,1)S(1)}, bf16[192,2,2,128]{3,2,1,0:T(2,128)(2,1)S(1)}, u32[]{:S(2)}, u32[]{:S(2)}) collective-permute-start(bf16[192,2,2,128]{3,2,1,0:T(2,128)(2,1)S(1)} %collective-permute-done.4.refs_2_), channel_id=1, source_target_pairs={{0,4},{4,0},{8,12},{12,8},{1,5},{5,1},{9,13},{13,9},{2,6},{6,2},{1... | collective-permute-start | bytes 589832 | tf_op jit(solution)/shard_map/ppermute | solution.py:33
  15.3 11.9 %collective-permute-start.1 = (bf16[104,2,128]{2,1,0:T(2,128)(2,1)S(1)}, bf16[104,2,128]{2,1,0:T(2,128)(2,1)S(1)}, u32[]{:S(2)}, u32[]{:S(2)}) collective-permute-start(bf16[104,2,128]{2,1,0:T(2,128)(2,1)S(1)} %get-tuple-element.45), channel_id=1, source_target_pairs={{0,8},{4,12},{8,0},{12,4},{1,9},{5,13},{9,1},{13,5},{2,10},{6,14},... | collective-permute-start | bytes 159752 | tf_op jit(solution)/shard_map/ppermute | solution.py:33
  17.4 9.8 %copy-start.4 = (bf16[1040,128]{1,0:T(8,128)(2,1)S(1)}, bf16[1040,128]{1,0:T(8,128)(2,1)}, u32[]{:S(2)}) copy-start(bf16[1040,128]{1,0:T(8,128)(2,1)} %get-tuple-element.23) | copy-start | bytes 798724
  22.7 15.0 %collective-permute-start.8 = (bf16[1040,128]{1,0:T(8,128)(2,1)S(1)}, bf16[1040,128]{1,0:T(8,128)(2,1)S(1)}, u32[]{:S(2)}, u32[]{:S(2)}) collective-permute-start(bf16[1040,128]{1,0:T(8,128)(2,1)S(1)} %collective-permute-done.7.refs_2_), channel_id=1, source_target_pairs={{0,4},{4,0},{8,12},{12,8},{1,5},{5,1},{9,13},{13,9},{2,6},{6,2},{1... | collective-permute-start | bytes 798728 | tf_op jit(solution)/shard_map/ppermute | solution.py:33
  27.2 14.9 %collective-permute-start.6 = (bf16[1040,128]{1,0:T(8,128)(2,1)S(1)}, bf16[1040,128]{1,0:T(8,128)(2,1)S(1)}, u32[]{:S(2)}, u32[]{:S(2)}) collective-permute-start(bf16[1040,128]{1,0:T(8,128)(2,1)S(1)} %copy-done.4), channel_id=1, source_target_pairs={{0,8},{4,12},{8,0},{12,4},{1,9},{5,13},{9,1},{13,5},{2,10},{6,14},... | collective-permute-start | bytes 798728 | tf_op jit(solution)/shard_map/ppermute | solution.py:33
  29.0 7.1 %copy-start.5 = (bf16[1024,128]{1,0:T(8,128)(2,1)S(1)}, bf16[1024,128]{1,0:T(8,128)(2,1)}, u32[]{:S(2)}) copy-start(bf16[1024,128]{1,0:T(8,128)(2,1)} %get-tuple-element.32) | copy-start | bytes 786436
  36.1 1.5 %collective-permute-start.10 = (bf16[1024,128]{1,0:T(8,128)(2,1)S(1)}, bf16[1024,128]{1,0:T(8,128)(2,1)S(1)}, u32[]{:S(2)}, u32[]{:S(2)}) collective-permute-start(bf16[1024,128]{1,0:T(8,128)(2,1)S(1)} %collective-permute-done.9.refs_4_), channel_id=1, source_target_pairs={{0,4},{4,0},{8,12},{12,8},{1,5},{5,1},{9,13},{13,9},{2,6},{6,2},{1... | collective-permute-start | bytes 786440 | tf_op jit(solution)/shard_map/ppermute | solution.py:33
  36.1 8.7 %collective-permute-start.12 = (bf16[1024,128]{1,0:T(8,128)(2,1)S(1)}, bf16[1024,128]{1,0:T(8,128)(2,1)S(1)}, u32[]{:S(2)}, u32[]{:S(2)}) collective-permute-start(bf16[1024,128]{1,0:T(8,128)(2,1)S(1)} %copy-done.5), channel_id=1, source_target_pairs={{0,8},{4,12},{8,0},{12,4},{1,9},{5,13},{9,1},{13,5},{2,10},{6,14},... | collective-permute-start | bytes 786440 | tf_op jit(solution)/shard_map/ppermute | solution.py:33
  42.2 4.2 %collective-permute-start.11 = (bf16[1040,128]{1,0:T(8,128)(2,1)S(1)}, bf16[1040,128]{1,0:T(8,128)(2,1)S(1)}, u32[]{:S(2)}, u32[]{:S(2)}) collective-permute-start(bf16[1040,128]{1,0:T(8,128)(2,1)S(1)} %collective-permute-done.6.refs_0_), channel_id=1, source_target_pairs={{0,4},{4,0},{8,12},{12,8},{1,5},{5,1},{9,13},{13,9},{2,6},{6,2},{1... | collective-permute-start | bytes 798728 | tf_op jit(solution)/shard_map/ppermute | solution.py:33
  44.8 1.5 %collective-permute-start.13 = (bf16[1024,128]{1,0:T(8,128)(2,1)S(1)}, bf16[1024,128]{1,0:T(8,128)(2,1)S(1)}, u32[]{:S(2)}, u32[]{:S(2)}) collective-permute-start(bf16[1024,128]{1,0:T(8,128)(2,1)S(1)} %collective-permute-done.12.refs_2_), channel_id=1, source_target_pairs={{0,4},{4,0},{8,12},{12,8},{1,5},{5,1},{9,13},{13,9},{2,6},{6,2},{1... | collective-permute-start | bytes 786440 | tf_op jit(solution)/shard_map/ppermute | solution.py:33
where the time goes:
time: 51.7 us; the launch traced here: 51.5 us
  Pallas kernels  24.7 us (48%)
  waiting for transfers between devices  11.8 us (23%)
  starting transfers between devices  10.2 us (20%)
  local copies, waits for them, and re-layouts  2.96 us (6%)
  between operations  1.59 us (3%)
    ppermute x14, waiting for transfers between devices, swap(): lax.ppermute(value, AXIS, [(one, one ^ distance) for one in range(count)])  11.8 us
    ppermute x14, starting transfers between devices, swap(): lax.ppermute(value, AXIS, [(one, one ^ distance) for one in range(count)])  10.2 us
    pallas_call x2, Pallas kernels, far_sums(): pl.pallas_call(functools.partial(far_kernel, head, group, count, rows //...  9.45 us
    pallas_call x1, Pallas kernels, key_sums(): pl.pallas_call(functools.partial(keys_kernel, slots, group, steps, span),...  7.12 us
    pallas_call x1, Pallas kernels, near_sums(): pl.pallas_call(functools.partial(near_kernel, span, states), out_shape=ja...  5.23 us
    pallas_call x1, Pallas kernels, pick_rows(): pl.pallas_call(pick_kernel, out_shape=[jax.ShapeDtypeStruct((steps,) + pa...  2.93 us
    squeeze x2, local copies, waits for them, and re-layouts, on_device(): prior_state[head, first:stop]  2.69 us
  transfers between devices with their start and end apart: 14, of which 5 were waited for; matrix products, arithmetic and copies ran while one was open for 6% of the time, Pallas kernels for 38%

commit v1 on v0

--- a/solution.py
+++ b/solution.py
@@ -203,12 +203,23 @@
     return jnp.swapaxes(value, 0, 1)
 
 
-def near_kernel(span, states, info_ref, q_ref, *refs):
+def inverse_root(ref, group, first):
+    row = lax.broadcasted_iota(jnp.int32, ref.shape, 0).astype(jnp.float32)
+    token = jnp.floor((row + 0.5) * (1.0 / group))
+    ref[...] = 1.0 / jnp.sqrt(token + first.astype(jnp.float32))
+
+
+def near_kernel(span, states, group, count, info_ref, q_ref, *refs):
     ins = refs[: len(states.arrays)]
-    sum_ref = refs[len(states.arrays)]
-    scratch = refs[len(states.arrays) + 1 :]
+    sum_ref, by_ref, root_ref, step_root_ref = refs[len(states.arrays) : len(states.arrays) + 4]
+    scratch = refs[len(states.arrays) + 4 :]
     copies = states.bring(ins, scratch, info_ref)
     query = by_head(q_ref[...])
+    by_ref[...] = query
+    tokens = query.shape[1] // group
+    start = info_ref[count + 1] + 1
+    inverse_root(root_ref, group, start + info_ref[0] * tokens)
+    inverse_root(step_root_ref, group, start + count * tokens + info_ref[count])
     first_block = span.first_block(info_ref[0])
     for copy in copies:
         copy.wait()
@@ -216,13 +227,18 @@
         carried(query[head], scratch[head], span, first_block, sum_ref.at[head], True)
 
 
-def near_sums(info, query, span, states):
+def near_sums(info, query, span, states, step_rows, group, count):
     rows, heads, width = query.shape
     return pl.pallas_call(
-        functools.partial(near_kernel, span, states),
-        out_shape=jax.ShapeDtypeStruct((heads, rows, width), jnp.float32),
+        functools.partial(near_kernel, span, states, group, count),
+        out_shape=[
+            jax.ShapeDtypeStruct((heads, rows, width), jnp.float32),
+            jax.ShapeDtypeStruct((heads, rows, width), query.dtype),
+            jax.ShapeDtypeStruct((rows, width), jnp.float32),
+            jax.ShapeDtypeStruct((step_rows, width), jnp.float32),
+        ],
         in_specs=[IN_SMEM, IN_VMEM] + [ANYWHERE] * len(states.arrays),
-        out_specs=IN_VMEM,
+        out_specs=[IN_VMEM] * 4,
         scratch_shapes=states.scratch(),
         compiler_params=params(),
         cost_estimate=cost(),
@@ -257,10 +273,9 @@
     kv_refs = refs[:slots]
     sum_ref, step_ref, f_ref, state_ref, rows_ref = refs[slots:]
     f_ref[...] = mine_ref[...] + theirs_ref[...]
-    rows, heads, width = q_ref.shape
+    heads, rows, width = q_ref.shape
     step_rows = step_ref.shape[1]
     me = info_ref[0]
-    query = by_head(q_ref[...])
     step_query, step_pairs = step_parts(f_ref, heads, step_rows, steps)
     first_block = span.first_block(me)
     keys = kv_refs[0].shape[0]
@@ -280,7 +295,7 @@
             bound = jnp.where(column < keys, column * group, 0) if start == 0 else column * 0
             part_keys = jnp.concatenate([pair[0] for pair in part], 0)
             part_values = jnp.concatenate([pair[1] for pair in part], 0)
-            total = total + squared_sum(query[head], part_keys, part_values, scale, bound)
+            total = total + squared_sum(q_ref[head], part_keys, part_values, scale, bound)
             full = jnp.full(column.shape, unit, jnp.float32)
             added = squared_sum(step_query[head], part_keys, part_values, full, column * 0)
             steps_total = added if steps_total is None else steps_total + added
@@ -306,7 +321,7 @@
 
 
 def key_sums(info, query, mine, theirs, prior, near, pairs, step_rows, steps, group, span):
-    rows, heads, width = query.shape
+    heads, rows, width = query.shape
     slots = len(pairs)
     state_shape = prior.shape if span.aligned else (heads,) + span.shape
     return pl.pallas_call(
@@ -325,23 +340,23 @@
     )(info, query, mine, theirs, prior, near, *[pairs[slot] for slot in range(slots)])
 
 
-def far_kernel(head, group, count, tokens, span, states, outputs, info_ref, q_ref, f_ref, *refs):
+def far_kernel(head, count, span, states, outputs, info_ref, q_ref, f_ref, *refs):
     ins, refs = refs[: len(states.arrays)], refs[len(states.arrays) :]
-    sum_ref, step_ref, refs = refs[0], refs[1], refs[2:]
+    sum_ref, step_ref, root_ref, step_root_ref = refs[:4]
+    refs = refs[4:]
     taken = 3 if head else 0
     earlier, refs = refs[:taken], refs[taken:]
     results, refs = refs[:outputs], refs[outputs:]
     total_ref, scratch = refs[0], refs[1 : 2 + len(states.plan)]
-    rows, heads, width = q_ref.shape
+    heads, rows, width = q_ref.shape
     step_rows = step_ref.shape[1]
     copies = states.bring(ins, scratch, info_ref)
-    query = by_head(q_ref[...])
     step_query = by_head(f_ref[:step_rows])
     first_block = span.first_block(info_ref[0])
     far_block = span.first_block(info_ref[count // 2])
     for copy in copies:
         copy.wait()
-    both = jnp.concatenate([query[head], step_query[head]], 0)
+    both = jnp.concatenate([q_ref[head], step_query[head]], 0)
     carried(both, scratch[len(states.plan) - 1], span, far_block, total_ref, True)
     if head:
         near_ref = earlier[2]
@@ -349,20 +364,11 @@
         near_ref = results[2] if heads > 1 else refs[-1]
         for one in range(heads):
             carried(step_query[one], scratch[one], span, first_block, near_ref.at[one], True)
-    start = info_ref[count + 1] + 1
-    found = []
-    for own, total, first in (
-        (sum_ref[head], total_ref[:rows], start + info_ref[0] * tokens),
-        (
-            step_ref[head],
-            total_ref[rows:] + near_ref[head],
-            start + count * tokens + info_ref[count],
-        ),
-    ):
-        row = lax.broadcasted_iota(jnp.int32, own.shape, 0).astype(jnp.float32)
-        token = jnp.floor((row + 0.5) * (1.0 / group))
-        position = token + first.astype(jnp.float32)
-        found.append((total * (1.0 / width) + own) / jnp.sqrt(position))
+    unit = 1.0 / width
+    found = [
+        (total_ref[:rows] * unit + sum_ref[head]) * root_ref[...],
+        ((total_ref[rows:] + near_ref[head]) * unit + step_ref[head]) * step_root_ref[...],
+    ]
     for at in range(2):
         if head < heads - 1:
             done = [earlier[at][one] for one in range(head)] + [found[at]]
@@ -373,8 +379,8 @@
             results[at][...] = jnp.stack(done, 1).astype(jnp.bfloat16)
 
 
-def far_sums(head, info, query, final, sums, step_sums, earlier, group, count, span, states):
-    rows, heads, width = query.shape
+def far_sums(head, info, query, final, sums, step_sums, roots, earlier, count, span, states):
+    heads, rows, width = query.shape
     step_rows = step_sums.shape[1]
     held = [pltpu.VMEM((rows + step_rows, width), jnp.float32)]
     near = jax.ShapeDtypeStruct((heads, step_rows, width), jnp.float32)
@@ -390,19 +396,17 @@
         ] + ([near] if head == 0 else [])
     spare = [pltpu.VMEM(near.shape, near.dtype)] if heads == 1 else []
     return pl.pallas_call(
-        functools.partial(
-            far_kernel, head, group, count, rows // group, span, states, len(shapes)
-        ),
+        functools.partial(far_kernel, head, count, span, states, len(shapes)),
         out_shape=shapes,
         in_specs=[IN_SMEM]
         + [IN_VMEM] * 2
         + [ANYWHERE] * len(states.arrays)
-        + [IN_VMEM] * (2 + len(earlier)),
+        + [IN_VMEM] * (4 + len(earlier)),
         out_specs=[IN_VMEM] * len(shapes),
         scratch_shapes=held + states.scratch() + spare,
         compiler_params=params(),
         cost_estimate=cost(),
-    )(info, query, final, *states.arrays, sums, step_sums, *earlier)
+    )(info, query, final, *states.arrays, sums, step_sums, *roots, *earlier)
 
 
 def on_device(queries, keys_values, prior_state, counts, continuation, query_table, pair_table):
@@ -420,12 +424,10 @@
     pairs = gather_all(keys_values, [far] + nearer)
     near_prior = gather_all(prior_state, nearer)
 
-    half = shard_rows // 2
-    half = round_up(half, 16) if shard_rows % 16 == 0 else half
-    cuts = [(0, half), (half, shard_rows)]
-    parts = [(head, first, prior_state[head, first:stop]) for head in range(heads) for first, stop in cuts]
-    opening, continuation = lax.optimization_barrier((parts[0][2], continuation))
-    parts[0] = (0, 0, opening)
+    parts = [prior_state[head] for head in range(heads)]
+    opening, _ = lax.optimization_barrier((parts[0], pairs[far]))
+    arrived = [swap(opening, far)]
+    continuation, _ = lax.optimization_barrier((continuation, parts))
 
     picked = pick_rows(
         info, continuation, jnp.transpose(query_table, (0, 2, 1, 3)), pair_table
@@ -442,15 +444,13 @@
 
     outgoing = share(me ^ far)
     mine, theirs = share(me), swap(outgoing, far)
-    arrived = [swap(opening, far)]
-    for head, first, rows in parts[1:]:
+    for rows in parts[1:]:
         rows, _ = lax.optimization_barrier((rows, outgoing))
         arrived.append(swap(rows, far))
 
-    def passed_on(at, after):
-        head, first, _ = parts[at]
-        rows, _ = lax.optimization_barrier((arrived[at], after))
-        return [(slot ^ far, first, part) for slot, part in sorted(gather_all(rows, nearer).items())]
+    def passed_on(head, after):
+        rows, _ = lax.optimization_barrier((arrived[head], after))
+        return [(slot ^ far, 0, part) for slot, part in sorted(gather_all(rows, nearer).items())]
 
     query = jnp.transpose(queries, (0, 2, 1, 3)).reshape(tokens * group, heads, width)
     span = Span(far, count, shard_rows, width)
@@ -464,25 +464,27 @@
 
     near_held = [(slot, 0, rows) for slot, rows in sorted(near_prior.items())]
     near_pieces = [pieces(near_held, head) for head in range(heads)]
-    near = near_sums(info, query, span, States(span, near_pieces))
-    held = [passed_on(0, near)]
+    query, pairs = lax.optimization_barrier((query, pairs))
+    near, query, *roots = near_sums(
+        info, query, span, States(span, near_pieces), step_rows, group, count
+    )
     sums, step_sums, final, decode_state = key_sums(
         info, query, mine, theirs, prior_state, near, pairs, step_rows, steps, group, own_span
     )
-    held.append(passed_on(1, sums))
+    held = [passed_on(0, (near, theirs))]
     if not own_span.aligned:
         added = lax.dynamic_slice_in_dim(decode_state, own_span.spot(me), shard_rows, 1)
         decode_state = prior_state.astype(jnp.float32) + added
     earlier = []
     for head in range(heads):
-        far_pieces = pieces(held[2 * head] + held[2 * head + 1], head)
+        far_pieces = pieces(held[head], head)
         states = States(span, (near_pieces if head == 0 else []) + [far_pieces])
         found = far_sums(
-            head, info, query, final, sums, step_sums, earlier, group, count, span, states
+            head, info, query, final, sums, step_sums, roots, earlier, count, span, states
         )
         earlier = list(found[:2]) + (earlier[2:] if head else list(found[2:]))
         if head < heads - 1:
-            held += [passed_on(2 * head + 2, found[0]), passed_on(2 * head + 3, found[0])]
+            held.append(passed_on(head + 1, found[0]))
     readout, decode_out = earlier[:2]
     readout = jnp.transpose(readout.reshape(tokens, group, heads, width), (0, 2, 1, 3))
     decode_out = jnp.transpose(decode_out.reshape(own_steps, group, heads, width), (0, 2, 1, 3))

time: 51.7 us -> 46.9 us (0.907)
  starting transfers between devices: 10.2 us -> 5.99 us
  waiting for transfers between devices: 11.8 us -> 10.5 us
  other arithmetic: 0.23 us -> 1.12 us
    ppermute x14 -> x10, starting transfers between devices: 10.2 us -> 5.99 us  [swap(): lax.ppermute(value, AXIS, [(one, one ^ distance) for one in range(count)])]
    ppermute x14 -> x10, waiting for transfers between devices: 11.8 us -> 10.5 us  [swap(): lax.ppermute(value, AXIS, [(one, one ^ distance) for one in range(count)])]
    add x1, other arithmetic: 0.12 us -> 1.02 us  [on_device(): picked = picked + swap(picked, step)]
    squeeze x2 -> x1, local copies, waits for them, and re-layouts: 2.69 us -> 2.26 us  [on_device(): parts = [prior_state[head] for head in range(heads)]]
  transfers between devices with their start and end apart: 14 -> 10, of which waited for: 5 -> 4; matrix products, arithmetic and copies ran while one was open for 6% -> 8% of each run, Pallas kernels for 38% -> 43%
where the time goes in v1:
time: 46.9 us; the launch traced here: 46.6 us
  Pallas kernels  24.9 us (53%)
  waiting for transfers between devices  10.5 us (22%)
  starting transfers between devices  5.99 us (13%)
  local copies, waits for them, and re-layouts  2.51 us (5%)
  between operations  1.56 us (3%)
  other arithmetic  1.12 us (2%)
    ppermute x10, waiting for transfers between devices, swap(): lax.ppermute(value, AXIS, [(one, one ^ distance) for one in range(count)])  10.5 us
    pallas_call x2, Pallas kernels, far_sums(): pl.pallas_call(functools.partial(far_kernel, head, count, span, states, l...  9.03 us
    pallas_call x1, Pallas kernels, key_sums(): pl.pallas_call(functools.partial(keys_kernel, slots, group, steps, span),...  7.49 us
    ppermute x10, starting transfers between devices, swap(): lax.ppermute(value, AXIS, [(one, one ^ distance) for one in range(count)])  5.99 us
    pallas_call x1, Pallas kernels, near_sums(): pl.pallas_call(functools.partial(near_kernel, span, states, group, count)...  5.53 us
    pallas_call x1, Pallas kernels, pick_rows(): pl.pallas_call(pick_kernel, out_shape=[jax.ShapeDtypeStruct((steps,) + pa...  2.86 us
    squeeze x1, local copies, waits for them, and re-layouts, on_device(): parts = [prior_state[head] for head in range(heads)]  2.26 us
    add x1, other arithmetic, on_device(): picked = picked + swap(picked, step)  1.02 us
  transfers between devices with their start and end apart: 10, of which 4 were waited for; matrix products, arithmetic and copies ran while one was open for 8% of the time, Pallas kernels for 43%

profile of v1, /device:TPU:0, one launch (start us, length us, event | category | flops | bytes accessed | tf_op | source)
XLA Modules:
  0.0 46.6 jit_solution(2757549918852814222)
XLA Ops:
  0.6 0.0 copy-start.3
  0.6 3.0 %collective-permute-start.1 = (bf16[192,2,2,128]{3,2,1,0:T(2,128)(2,1)}, bf16[192,2,2,128]{3,2,1,0:T(2,128)(2,1)}, u32[]{:S(2)}, u32[]{:S(2)}) collective-permute-start(bf16[192,2,2,128]{3,2,1,0:T(2,128)(2,1)} %refs_0_.3), channel_id=1, source_target_pairs={{0,8},{4,12},{8,0},{12,4},{1,9},{5,13},{9,1},{13,5},{2,10},{6,14},... | collective-permute-start | bytes 589832 | tf_op jit(solution)/shard_map/ppermute | solution.py:33
  3.6 0.0 collective-permute-start.3
  3.6 2.3 %slice_bitcast_fusion = (bf16[2064,128]{1,0:T(8,128)(2,1)}, bf16[2064,128]{1,0:T(8,128)(2,1)}) fusion(bf16[2,2064,128]{2,1,0:T(8,128)(2,1)} %refs_0_.4), kind=kLoop, calls=%fused_computation | loop fusion | bytes 2113536 | tf_op jit(solution)/shard_map/squeeze | solution.py:427
  6.6 0.1 stack.23.info_ref
  6.6 0.0 copy-done.3
  6.6 0.0 copy-start.2
  6.6 0.0 copy-start
  6.7 0.0 copy-start.1
  6.7 2.9 %shard_map.95 = bf16[32,7,2,128]{3,2,1,0:T(2,128)(2,1)S(1)} custom-call(s32[6]{0:T(128)S(1)} %stack.23.info_ref, s32[32]{0:T(128)S(1)} %copy-done.3, bf16[18992,5,2,128]{3,2,1,0:T(2,128)(2,1)} %bitcast.25, bf16[18992,2,2,128]{3,2,1,0:T(2,128)(2,1)} %pt_ref.1), custom_call_target="tpu_custom_call" | custom-call | flops 1024 | bytes 1024 | tf_op jit(solution)/shard_map/pallas_call | solution.py:87
  9.5 0.4 collective-permute-start.4
  9.9 0.0 collective-permute-done.1.refs_2_
  9.9 0.7 %collective-permute-start.7 = (bf16[2064,128]{1,0:T(8,128)(2,1)}, bf16[2064,128]{1,0:T(8,128)(2,1)S(1)}, u32[]{:S(2)}, u32[]{:S(2)}) collective-permute-start(bf16[2064,128]{1,0:T(8,128)(2,1)} %get-tuple-element.36), channel_id=1, source_target_pairs={{0,8},{4,12},{8,0},{12,4},{1,9},{5,13},{9,1},{13,5},{2,10},{6,14},... | collective-permute-start | bytes 1585160 | tf_op jit(solution)/shard_map/ppermute | solution.py:33
  10.6 0.0 copy-done.2
  10.6 0.0 collective-permute-start
  10.6 0.0 copy-start.4
  10.6 0.5 collective-permute-done.4
  11.1 1.0 %add.9 = bf16[32,7,2,128]{3,2,1,0:T(2,128)(2,1)S(1)} add(bf16[32,7,2,128]{3,2,1,0:T(2,128)(2,1)S(1)} %shard_map.95, bf16[32,7,2,128]{3,2,1,0:T(2,128)(2,1)} %collective-permute-done.4) | non-fusion elementwise | flops 57344 | bytes 344064 | tf_op jit(solution)/shard_map/add | solution.py:436
  12.1 0.1 slice.18
  12.2 0.4 collective-permute-start.2
  12.6 0.1 pad_maximum_fusion.1
  12.7 1.2 %collective-permute-start.5 = (bf16[104,2,128]{2,1,0:T(2,128)(2,1)S(1)}, bf16[104,2,128]{2,1,0:T(2,128)(2,1)S(1)}, u32[]{:S(2)}, u32[]{:S(2)}) collective-permute-start(bf16[104,2,128]{2,1,0:T(2,128)(2,1)S(1)} %get-tuple-element.53), channel_id=1, source_target_pairs={{0,8},{4,12},{8,0},{12,4},{1,9},{5,13},{9,1},{13,5},{2,10},{6,14},... | collective-permute-start | bytes 159752 | tf_op jit(solution)/shard_map/ppermute | solution.py:33
  13.9 0.0 collective-permute-done.refs_1_
  13.9 0.0 collective-permute-done.2.refs_3_
  13.9 0.0 collective-permute-done.3.refs_1_
  14.0 0.0 copy-done
  14.0 0.0 copy-done.1
  14.0 5.5 %shard_map.94 = (f32[2,960,128]{2,1,0:T(8,128)S(1)}, bf16[2,960,128]{2,1,0:T(8,128)(2,1)S(1)}, f32[960,128]{1,0:T(8,128)S(1)}, f32[40,128]{1,0:T(8,128)S(1)}) custom-call(s32[6]{0:T(128)S(1)} %stack.23.info_ref, bf16[960,2,128]{2,1,0:T(2,128)(2,1)S(1)} %bitcast.24, bf16[2,2064,128]{2,1,0:T(8,128)(2,1)S(1)} %copy-done, ...), custom_call_target="tpu_custom_call" | custom-call | flops 1024 | bytes 1024 | tf_op jit(solution)/shard_map/pallas_call | solution.py:232
  19.5 5.9 %collective-permute-done.5.theirs_ref = bf16[104,2,128]{2,1,0:T(2,128)(2,1)S(1)} collective-permute-done((bf16[104,2,128]{2,1,0:T(2,128)(2,1)S(1)}, bf16[104,2,128]{2,1,0:T(2,128)(2,1)S(1)}, u32[]{:S(2)}, u32[]{:S(2)}) %collective-permute-start.5) | collective-permute-done | bytes 53280 | tf_op jit(solution)/shard_map/ppermute | solution.py:33
  25.4 0.0 collective-permute-done.7.refs_2_
  25.4 0.0 collective-permute-start.8
  25.4 0.0 copy-done.4
  25.4 0.3 collective-permute-start.6
  25.8 7.5 %shard_map.96 = (f32[2,960,128]{2,1,0:T(8,128)S(1)}, f32[2,40,128]{2,1,0:T(8,128)S(1)}, bf16[104,2,128]{2,1,0:T(2,128)(2,1)S(1)}, f32[2,2064,128]{2,1,0:T(8,128)}) custom-call(s32[6]{0:T(128)S(1)} %stack.23.info_ref, bf16[2,960,128]{2,1,0:T(8,128)(2,1)S(1)} %get-tuple-element.27.q_ref, bf16[104,2,128]{2,1,0:T(2,128)(2,1)S(1)} %get-tuple-element.54.mine_ref, ...), custom_call_target="tpu_custom_call" | custom-call | flops 1024 | bytes 1024 | tf_op jit(solution)/shard_map/pallas_call | solution.py:327
  33.2 0.0 collective-permute-done.8.refs_3_
  33.2 4.4 %shard_map.97 = (f32[1,960,128]{2,1,0:T(8,128)S(1)}, f32[1,40,128]{2,1,0:T(8,128)S(1)}, f32[2,40,128]{2,1,0:T(8,128)S(1)}) custom-call(s32[6]{0:T(128)S(1)} %stack.23.info_ref, bf16[2,960,128]{2,1,0:T(8,128)(2,1)S(1)} %get-tuple-element.27.q_ref, bf16[104,2,128]{2,1,0:T(2,128)(2,1)S(1)} %get-tuple-element.34.f_ref, bf16[2,2064,128]{2,1,0:T(8,128)(2,1)S(1)} %copy-done, ...), custom_call_target="tpu_custom_call" | custom-call | flops 1024 | bytes 1024 | tf_op jit(solution)/shard_map/pallas_call | solution.py:398
  37.6 2.2 %collective-permute-done.6.refs_0_ = bf16[2064,128]{1,0:T(8,128)(2,1)S(1)} collective-permute-done((bf16[2064,128]{1,0:T(8,128)(2,1)S(1)}, bf16[2064,128]{1,0:T(8,128)(2,1)S(1)}, u32[]{:S(2)}, u32[]{:S(2)}) %collective-permute-start.6) | collective-permute-done | bytes 528416 | tf_op jit(solution)/shard_map/ppermute | solution.py:33
  39.8 0.0 collective-permute-start.9
  39.8 1.9 %collective-permute-done.9.refs_1_ = bf16[2064,128]{1,0:T(8,128)(2,1)S(1)} collective-permute-done((bf16[2064,128]{1,0:T(8,128)(2,1)S(1)}, bf16[2064,128]{1,0:T(8,128)(2,1)S(1)}, u32[]{:S(2)}, u32[]{:S(2)}) %collective-permute-start.9) | collective-permute-done | bytes 528416 | tf_op jit(solution)/shard_map/ppermute | solution.py:33
  41.7 4.7 %shard_map.98 = (bf16[960,2,128]{2,1,0:T(2,128)(2,1)}, bf16[40,2,128]{2,1,0:T(2,128)(2,1)}) custom-call(s32[6]{0:T(128)S(1)} %stack.23.info_ref, bf16[2,960,128]{2,1,0:T(8,128)(2,1)S(1)} %get-tuple-element.27.q_ref, bf16[104,2,128]{2,1,0:T(2,128)(2,1)S(1)} %get-tuple-element.34.f_ref, bf16[2064,128]{1,0:T(8,128)(2,1)S(1)} %collective-permute-done.6.refs_0_, ...), custom_call_target="tpu_custom_call" | custom-call | flops 1024 | bytes 1024 | tf_op jit(solution)/shard_map/pallas_call | solution.py:398
  (3 shorter events, 0.1 us)
Async XLA Ops:
  0.6 6.0 %copy-start.3 = (s32[32]{0:T(128)S(1)}, s32[32]{0:T(128)}, u32[]{:S(2)}) copy-start(s32[32]{0:T(128)} %ids_ref) | copy-start | bytes 388
  0.6 9.3 %collective-permute-start.1 = (bf16[192,2,2,128]{3,2,1,0:T(2,128)(2,1)}, bf16[192,2,2,128]{3,2,1,0:T(2,128)(2,1)}, u32[]{:S(2)}, u32[]{:S(2)}) collective-permute-start(bf16[192,2,2,128]{3,2,1,0:T(2,128)(2,1)} %refs_0_.3), channel_id=1, source_target_pairs={{0,8},{4,12},{8,0},{12,4},{1,9},{5,13},{9,1},{13,5},{2,10},{6,14},... | collective-permute-start | bytes 589832 | tf_op jit(solution)/shard_map/ppermute | solution.py:33
  3.6 10.3 %collective-permute-start.3 = (bf16[2,2064,128]{2,1,0:T(8,128)(2,1)}, bf16[2,2064,128]{2,1,0:T(8,128)(2,1)S(1)}, u32[]{:S(2)}, u32[]{:S(2)}) collective-permute-start(bf16[2,2064,128]{2,1,0:T(8,128)(2,1)} %refs_0_.4), channel_id=1, source_target_pairs={{0,4},{4,0},{8,12},{12,8},{1,5},{5,1},{9,13},{13,9},{2,6},{6,2},{1... | collective-permute-start | bytes 3170312 | tf_op jit(solution)/shard_map/ppermute | solution.py:33
  6.6 4.0 %copy-start.2 = (bf16[192,2,2,128]{3,2,1,0:T(2,128)(2,1)S(1)}, bf16[192,2,2,128]{3,2,1,0:T(2,128)(2,1)}, u32[]{:S(2)}) copy-start(bf16[192,2,2,128]{3,2,1,0:T(2,128)(2,1)} %refs_0_.3) | copy-start | bytes 589828
  6.6 7.3 %copy-start = (bf16[2,2064,128]{2,1,0:T(8,128)(2,1)S(1)}, bf16[2,2064,128]{2,1,0:T(8,128)(2,1)}, u32[]{:S(2)}) copy-start(bf16[2,2064,128]{2,1,0:T(8,128)(2,1)} %refs_0_.4) | copy-start | bytes 3170308
  6.7 7.3 %copy-start.1 = (bf16[192,2,5,128]{3,1,2,0:T(2,128)(2,1)S(1)}, bf16[192,2,5,128]{3,1,2,0:T(2,128)(2,1)}, u32[]{:S(2)}) copy-start(bf16[192,2,5,128]{3,1,2,0:T(2,128)(2,1)} %param.7) | copy-start | bytes 1474564
  9.5 1.5 %collective-permute-start.4 = (bf16[32,7,2,128]{3,2,1,0:T(2,128)(2,1)S(1)}, bf16[32,7,2,128]{3,2,1,0:T(2,128)(2,1)}, u32[]{:S(2)}, u32[]{:S(2)}) collective-permute-start(bf16[32,7,2,128]{3,2,1,0:T(2,128)(2,1)S(1)} %shard_map.95), channel_id=1, source_target_pairs={{0,4},{4,0},{8,12},{12,8},{1,5},{5,1},{9,13},{13,9},{2,6},{6,2},{1... | collective-permute-start | bytes 344072 | tf_op jit(solution)/shard_map/ppermute | solution.py:33
  9.9 15.5 %collective-permute-start.7 = (bf16[2064,128]{1,0:T(8,128)(2,1)}, bf16[2064,128]{1,0:T(8,128)(2,1)S(1)}, u32[]{:S(2)}, u32[]{:S(2)}) collective-permute-start(bf16[2064,128]{1,0:T(8,128)(2,1)} %get-tuple-element.36), channel_id=1, source_target_pairs={{0,8},{4,12},{8,0},{12,4},{1,9},{5,13},{9,1},{13,5},{2,10},{6,14},... | collective-permute-start | bytes 1585160 | tf_op jit(solution)/shard_map/ppermute | solution.py:33
  10.6 3.3 %collective-permute-start = (bf16[192,2,2,128]{3,2,1,0:T(2,128)(2,1)S(1)}, bf16[192,2,2,128]{3,2,1,0:T(2,128)(2,1)}, u32[]{:S(2)}, u32[]{:S(2)}) collective-permute-start(bf16[192,2,2,128]{3,2,1,0:T(2,128)(2,1)S(1)} %copy-done.2), channel_id=1, source_target_pairs={{0,4},{4,0},{8,12},{12,8},{1,5},{5,1},{9,13},{13,9},{2,6},{6,2},{1... | collective-permute-start | bytes 589832 | tf_op jit(solution)/shard_map/ppermute | solution.py:33
  10.6 14.8 %copy-start.4 = (bf16[2064,128]{1,0:T(8,128)(2,1)S(1)}, bf16[2064,128]{1,0:T(8,128)(2,1)}, u32[]{:S(2)}) copy-start(bf16[2064,128]{1,0:T(8,128)(2,1)} %get-tuple-element.35) | copy-start | bytes 1585156
  12.2 1.8 %collective-permute-start.2 = (bf16[192,2,2,128]{3,2,1,0:T(2,128)(2,1)}, bf16[192,2,2,128]{3,2,1,0:T(2,128)(2,1)S(1)}, u32[]{:S(2)}, u32[]{:S(2)}) collective-permute-start(bf16[192,2,2,128]{3,2,1,0:T(2,128)(2,1)} %collective-permute-done.1.refs_2_), channel_id=1, source_target_pairs={{0,4},{4,0},{8,12},{12,8},{1,5},{5,1},{9,13},{13,9},{2,6},{6,2},{1... | collective-permute-start | bytes 589832 | tf_op jit(solution)/shard_map/ppermute | solution.py:33
  12.7 12.7 %collective-permute-start.5 = (bf16[104,2,128]{2,1,0:T(2,128)(2,1)S(1)}, bf16[104,2,128]{2,1,0:T(2,128)(2,1)S(1)}, u32[]{:S(2)}, u32[]{:S(2)}) collective-permute-start(bf16[104,2,128]{2,1,0:T(2,128)(2,1)S(1)} %get-tuple-element.53), channel_id=1, source_target_pairs={{0,8},{4,12},{8,0},{12,4},{1,9},{5,13},{9,1},{13,5},{2,10},{6,14},... | collective-permute-start | bytes 159752 | tf_op jit(solution)/shard_map/ppermute | solution.py:33
  25.4 7.8 %collective-permute-start.8 = (bf16[2064,128]{1,0:T(8,128)(2,1)S(1)}, bf16[2064,128]{1,0:T(8,128)(2,1)S(1)}, u32[]{:S(2)}, u32[]{:S(2)}) collective-permute-start(bf16[2064,128]{1,0:T(8,128)(2,1)S(1)} %collective-permute-done.7.refs_2_), channel_id=1, source_target_pairs={{0,4},{4,0},{8,12},{12,8},{1,5},{5,1},{9,13},{13,9},{2,6},{6,2},{1... | collective-permute-start | bytes 1585160 | tf_op jit(solution)/shard_map/ppermute | solution.py:33
  25.4 14.4 %collective-permute-start.6 = (bf16[2064,128]{1,0:T(8,128)(2,1)S(1)}, bf16[2064,128]{1,0:T(8,128)(2,1)S(1)}, u32[]{:S(2)}, u32[]{:S(2)}) collective-permute-start(bf16[2064,128]{1,0:T(8,128)(2,1)S(1)} %copy-done.4), channel_id=1, source_target_pairs={{0,8},{4,12},{8,0},{12,4},{1,9},{5,13},{9,1},{13,5},{2,10},{6,14},... | collective-permute-start | bytes 1585160 | tf_op jit(solution)/shard_map/ppermute | solution.py:33
  39.8 1.9 %collective-permute-start.9 = (bf16[2064,128]{1,0:T(8,128)(2,1)S(1)}, bf16[2064,128]{1,0:T(8,128)(2,1)S(1)}, u32[]{:S(2)}, u32[]{:S(2)}) collective-permute-start(bf16[2064,128]{1,0:T(8,128)(2,1)S(1)} %collective-permute-done.6.refs_0_), channel_id=1, source_target_pairs={{0,4},{4,0},{8,12},{12,8},{1,5},{5,1},{9,13},{13,9},{2,6},{6,2},{1... | collective-permute-start | bytes 1585160 | tf_op jit(solution)/shard_map/ppermute | solution.py:33

commit v2 on v1

--- a/solution.py
+++ b/solution.py
@@ -424,10 +424,10 @@
     pairs = gather_all(keys_values, [far] + nearer)
     near_prior = gather_all(prior_state, nearer)
 
-    parts = [prior_state[head] for head in range(heads)]
-    opening, _ = lax.optimization_barrier((parts[0], pairs[far]))
+    opening = prior_state[0]
+    continuation, _ = lax.optimization_barrier((continuation, (opening, near_prior)))
+    opening, _ = lax.optimization_barrier((opening, pairs[far]))
     arrived = [swap(opening, far)]
-    continuation, _ = lax.optimization_barrier((continuation, parts))
 
     picked = pick_rows(
         info, continuation, jnp.transpose(query_table, (0, 2, 1, 3)), pair_table
@@ -444,9 +444,8 @@
 
     outgoing = share(me ^ far)
     mine, theirs = share(me), swap(outgoing, far)
-    for rows in parts[1:]:
-        rows, _ = lax.optimization_barrier((rows, outgoing))
-        arrived.append(swap(rows, far))
+    rest, _ = lax.optimization_barrier((prior_state, outgoing))
+    rest = [rest[head] for head in range(1, heads)]
 
     def passed_on(head, after):
         rows, _ = lax.optimization_barrier((arrived[head], after))
@@ -464,7 +463,8 @@
 
     near_held = [(slot, 0, rows) for slot, rows in sorted(near_prior.items())]
     near_pieces = [pieces(near_held, head) for head in range(heads)]
-    query, pairs = lax.optimization_barrier((query, pairs))
+    query, pairs, rest = lax.optimization_barrier((query, pairs, rest))
+    arrived += [swap(rows, far) for rows in rest]
     near, query, *roots = near_sums(
         info, query, span, States(span, near_pieces), step_rows, group, count
     )

time: 46.9 us -> 46.7 us (level)
  other arithmetic: 1.12 us -> 0.23 us
  waiting for transfers between devices: 10.5 us -> 11.3 us
  starting transfers between devices: 5.99 us -> 6.58 us
    add x1, other arithmetic: 1.02 us -> 0.12 us  [on_device(): picked = picked + swap(picked, step)]
    ppermute x10, waiting for transfers between devices: 10.5 us -> 11.3 us  [swap(): lax.ppermute(value, AXIS, [(one, one ^ distance) for one in range(count)])]
    ppermute x10, starting transfers between devices: 5.99 us -> 6.58 us  [swap(): lax.ppermute(value, AXIS, [(one, one ^ distance) for one in range(count)])]
    squeeze x1 -> x2, local copies, waits for them, and re-layouts: 2.26 us -> 1.91 us  [the longest x1 1.87 us: on_device(): opening = prior_state[0]]
  transfers between devices with their start and end apart: 10 -> 10, of which waited for: 4 -> 5; matrix products, arithmetic and copies ran while one was open for 8% -> 5% of each run, Pallas kernels for 43% -> 43%
where the time goes in v2:
time: 46.7 us; the launch traced here: 46.5 us
  Pallas kernels  24.6 us (53%)
  waiting for transfers between devices  11.3 us (24%)
  starting transfers between devices  6.58 us (14%)
  local copies, waits for them, and re-layouts  2.17 us (5%)
  between operations  1.58 us (3%)
    ppermute x10, waiting for transfers between devices, swap(): lax.ppermute(value, AXIS, [(one, one ^ distance) for one in range(count)])  11.3 us
    pallas_call x2, Pallas kernels, far_sums(): pl.pallas_call(functools.partial(far_kernel, head, count, span, states, l...  9.03 us
    pallas_call x1, Pallas kernels, key_sums(): pl.pallas_call(functools.partial(keys_kernel, slots, group, steps, span),...  7.08 us
    ppermute x10, starting transfers between devices, swap(): lax.ppermute(value, AXIS, [(one, one ^ distance) for one in range(count)])  6.58 us
    pallas_call x1, Pallas kernels, near_sums(): pl.pallas_call(functools.partial(near_kernel, span, states, group, count)...  5.52 us
    pallas_call x1, Pallas kernels, pick_rows(): pl.pallas_call(pick_kernel, out_shape=[jax.ShapeDtypeStruct((steps,) + pa...  2.96 us
    squeeze x1, local copies, waits for them, and re-layouts, on_device(): opening = prior_state[0]  1.87 us
  transfers between devices with their start and end apart: 10, of which 5 were waited for; matrix products, arithmetic and copies ran while one was open for 5% of the time, Pallas kernels for 43%

profile of v2, /device:TPU:0, one launch (start us, length us, event | category | flops | bytes accessed | tf_op | source)
XLA Modules:
  0.0 46.5 jit_solution(11411597481760791746)
XLA Ops:
  0.6 0.0 copy-start.3
  0.6 0.5 %collective-permute-start.3 = (bf16[2,2064,128]{2,1,0:T(8,128)(2,1)}, bf16[2,2064,128]{2,1,0:T(8,128)(2,1)S(1)}, u32[]{:S(2)}, u32[]{:S(2)}) collective-permute-start(bf16[2,2064,128]{2,1,0:T(8,128)(2,1)} %refs_0_.4), channel_id=1, source_target_pairs={{0,4},{4,0},{8,12},{12,8},{1,5},{5,1},{9,13},{13,9},{2,6},{6,2},{1... | collective-permute-start | bytes 3170312 | tf_op jit(solution)/shard_map/ppermute | solution.py:33
  1.2 2.6 %collective-permute-start.1 = (bf16[192,2,2,128]{3,2,1,0:T(2,128)(2,1)}, bf16[192,2,2,128]{3,2,1,0:T(2,128)(2,1)S(1)}, u32[]{:S(2)}, u32[]{:S(2)}) collective-permute-start(bf16[192,2,2,128]{3,2,1,0:T(2,128)(2,1)} %refs_0_.3), channel_id=1, source_target_pairs={{0,8},{4,12},{8,0},{12,4},{1,9},{5,13},{9,1},{13,5},{2,10},{6,14},... | collective-permute-start | bytes 589832 | tf_op jit(solution)/shard_map/ppermute | solution.py:33
  3.7 1.9 %slice_bitcast_fusion.1 = bf16[2064,128]{1,0:T(8,128)(2,1)} fusion(bf16[2,2064,128]{2,1,0:T(8,128)(2,1)} %refs_0_.4), kind=kLoop, calls=%fused_computation.1 | loop fusion | bytes 1056768 | tf_op jit(solution)/shard_map/squeeze | solution.py:427
  6.2 0.1 stack.23.info_ref
  6.3 0.0 collective-permute-done.3.refs_1_
  6.3 0.0 copy-done.3
  6.3 0.0 copy-start.2
  6.4 0.0 copy-start
  6.4 3.0 %shard_map.94 = bf16[32,7,2,128]{3,2,1,0:T(2,128)(2,1)S(1)} custom-call(s32[6]{0:T(128)S(1)} %stack.23.info_ref, s32[32]{0:T(128)S(1)} %copy-done.3, bf16[18992,5,2,128]{3,2,1,0:T(2,128)(2,1)} %bitcast.25, bf16[18992,2,2,128]{3,2,1,0:T(2,128)(2,1)} %pt_ref.1), custom_call_target="tpu_custom_call" | custom-call | flops 1024 | bytes 1024 | tf_op jit(solution)/shard_map/pallas_call | solution.py:87
  9.3 0.0 copy-start.1
  9.3 0.1 collective-permute-start.4
  9.4 0.0 copy-done.2
  9.4 0.5 %collective-permute-start = (bf16[192,2,2,128]{3,2,1,0:T(2,128)(2,1)S(1)}, bf16[192,2,2,128]{3,2,1,0:T(2,128)(2,1)S(1)}, u32[]{:S(2)}, u32[]{:S(2)}) collective-permute-start(bf16[192,2,2,128]{3,2,1,0:T(2,128)(2,1)S(1)} %copy-done.2), channel_id=1, source_target_pairs={{0,4},{4,0},{8,12},{12,8},{1,5},{5,1},{9,13},{13,9},{2,6},{6,2},{1... | collective-permute-start | bytes 589832 | tf_op jit(solution)/shard_map/ppermute | solution.py:33
  9.9 0.0 collective-permute-done.1.refs_2_
  9.9 1.3 %collective-permute-start.7 = (bf16[2064,128]{1,0:T(8,128)(2,1)}, bf16[2064,128]{1,0:T(8,128)(2,1)S(1)}, u32[]{:S(2)}, u32[]{:S(2)}) collective-permute-start(bf16[2064,128]{1,0:T(8,128)(2,1)} %slice_bitcast_fusion.1), channel_id=1, source_target_pairs={{0,8},{4,12},{8,0},{12,4},{1,9},{5,13},{9,1},{13,5},{2,10},{6,14},... | collective-permute-start | bytes 1585160 | tf_op jit(solution)/shard_map/ppermute | solution.py:33
  11.2 0.0 collective-permute-start.2
  11.2 0.0 collective-permute-done.4
  11.2 0.1 add.9
  11.3 0.1 slice.18
  11.5 0.1 pad_maximum_fusion.1
  11.6 0.8 %collective-permute-start.5 = (bf16[104,2,128]{2,1,0:T(2,128)(2,1)S(1)}, bf16[104,2,128]{2,1,0:T(2,128)(2,1)S(1)}, u32[]{:S(2)}, u32[]{:S(2)}) collective-permute-start(bf16[104,2,128]{2,1,0:T(2,128)(2,1)S(1)} %get-tuple-element.54), channel_id=1, source_target_pairs={{0,8},{4,12},{8,0},{12,4},{1,9},{5,13},{9,1},{13,5},{2,10},{6,14},... | collective-permute-start | bytes 159752 | tf_op jit(solution)/shard_map/ppermute | solution.py:33
  12.4 0.0 copy-done
  12.5 0.0 collective-permute-done.refs_1_
  12.5 0.1 collective-permute-done.2.refs_3_
  12.6 0.0 copy-done.1
  12.6 5.5 %shard_map.95 = (f32[2,960,128]{2,1,0:T(8,128)S(1)}, bf16[2,960,128]{2,1,0:T(8,128)(2,1)S(1)}, f32[960,128]{1,0:T(8,128)S(1)}, f32[40,128]{1,0:T(8,128)S(1)}) custom-call(s32[6]{0:T(128)S(1)} %stack.23.info_ref, bf16[960,2,128]{2,1,0:T(2,128)(2,1)S(1)} %bitcast.24, bf16[2,2064,128]{2,1,0:T(8,128)(2,1)S(1)} %copy-done, ...), custom_call_target="tpu_custom_call" | custom-call | flops 1024 | bytes 1024 | tf_op jit(solution)/shard_map/pallas_call | solution.py:232
  18.2 6.5 %collective-permute-done.7.refs_2_ = bf16[2064,128]{1,0:T(8,128)(2,1)S(1)} collective-permute-done((bf16[2064,128]{1,0:T(8,128)(2,1)}, bf16[2064,128]{1,0:T(8,128)(2,1)S(1)}, u32[]{:S(2)}, u32[]{:S(2)}) %collective-permute-start.7) | collective-permute-done | bytes 528416 | tf_op jit(solution)/shard_map/ppermute | solution.py:33
  24.7 0.6 %collective-permute-done.5.theirs_ref = bf16[104,2,128]{2,1,0:T(2,128)(2,1)S(1)} collective-permute-done((bf16[104,2,128]{2,1,0:T(2,128)(2,1)S(1)}, bf16[104,2,128]{2,1,0:T(2,128)(2,1)S(1)}, u32[]{:S(2)}, u32[]{:S(2)}) %collective-permute-start.5) | collective-permute-done | bytes 53280 | tf_op jit(solution)/shard_map/ppermute | solution.py:33
  25.3 0.0 collective-permute-start.8
  25.3 0.8 %collective-permute-start.6 = (bf16[2064,128]{1,0:T(8,128)(2,1)S(1)}, bf16[2064,128]{1,0:T(8,128)(2,1)S(1)}, u32[]{:S(2)}, u32[]{:S(2)}) collective-permute-start(bf16[2064,128]{1,0:T(8,128)(2,1)S(1)} %slice_bitcast_fusion), channel_id=1, source_target_pairs={{0,8},{4,12},{8,0},{12,4},{1,9},{5,13},{9,1},{13,5},{2,10},{6,14},... | collective-permute-start | bytes 1585160 | tf_op jit(solution)/shard_map/ppermute | solution.py:33
  26.1 7.1 %shard_map.96 = (f32[2,960,128]{2,1,0:T(8,128)S(1)}, f32[2,40,128]{2,1,0:T(8,128)S(1)}, bf16[104,2,128]{2,1,0:T(2,128)(2,1)S(1)}, f32[2,2064,128]{2,1,0:T(8,128)}) custom-call(s32[6]{0:T(128)S(1)} %stack.23.info_ref, bf16[2,960,128]{2,1,0:T(8,128)(2,1)S(1)} %get-tuple-element.30.q_ref, bf16[104,2,128]{2,1,0:T(2,128)(2,1)S(1)} %get-tuple-element.53.mine_ref, ...), custom_call_target="tpu_custom_call" | custom-call | flops 1024 | bytes 1024 | tf_op jit(solution)/shard_map/pallas_call | solution.py:327
  33.2 0.0 collective-permute-done.8.refs_3_
  33.2 4.4 %shard_map.97 = (f32[1,960,128]{2,1,0:T(8,128)S(1)}, f32[1,40,128]{2,1,0:T(8,128)S(1)}, f32[2,40,128]{2,1,0:T(8,128)S(1)}) custom-call(s32[6]{0:T(128)S(1)} %stack.23.info_ref, bf16[2,960,128]{2,1,0:T(8,128)(2,1)S(1)} %get-tuple-element.30.q_ref, bf16[104,2,128]{2,1,0:T(2,128)(2,1)S(1)} %get-tuple-element.36.f_ref, bf16[2,2064,128]{2,1,0:T(8,128)(2,1)S(1)} %copy-done, ...), custom_call_target="tpu_custom_call" | custom-call | flops 1024 | bytes 1024 | tf_op jit(solution)/shard_map/pallas_call | solution.py:398
  37.6 2.1 %collective-permute-done.6.refs_0_ = bf16[2064,128]{1,0:T(8,128)(2,1)S(1)} collective-permute-done((bf16[2064,128]{1,0:T(8,128)(2,1)S(1)}, bf16[2064,128]{1,0:T(8,128)(2,1)S(1)}, u32[]{:S(2)}, u32[]{:S(2)}) %collective-permute-start.6) | collective-permute-done | bytes 528416 | tf_op jit(solution)/shard_map/ppermute | solution.py:33
  39.7 0.0 collective-permute-start.9
  39.7 1.9 %collective-permute-done.9.refs_1_ = bf16[2064,128]{1,0:T(8,128)(2,1)S(1)} collective-permute-done((bf16[2064,128]{1,0:T(8,128)(2,1)S(1)}, bf16[2064,128]{1,0:T(8,128)(2,1)S(1)}, u32[]{:S(2)}, u32[]{:S(2)}) %collective-permute-start.9) | collective-permute-done | bytes 528416 | tf_op jit(solution)/shard_map/ppermute | solution.py:33
  41.6 4.7 %shard_map.98 = (bf16[960,2,128]{2,1,0:T(2,128)(2,1)}, bf16[40,2,128]{2,1,0:T(2,128)(2,1)}) custom-call(s32[6]{0:T(128)S(1)} %stack.23.info_ref, bf16[2,960,128]{2,1,0:T(8,128)(2,1)S(1)} %get-tuple-element.30.q_ref, bf16[104,2,128]{2,1,0:T(2,128)(2,1)S(1)} %get-tuple-element.36.f_ref, bf16[2064,128]{1,0:T(8,128)(2,1)S(1)} %collective-permute-done.6.refs_0_, ...), custom_call_target="tpu_custom_call" | custom-call | flops 1024 | bytes 1024 | tf_op jit(solution)/shard_map/pallas_call | solution.py:398
  (4 shorter events, 0.1 us)
Async XLA Ops:
  0.6 5.7 %copy-start.3 = (s32[32]{0:T(128)S(1)}, s32[32]{0:T(128)}, u32[]{:S(2)}) copy-start(s32[32]{0:T(128)} %ids_ref) | copy-start | bytes 388
  0.6 5.7 %collective-permute-start.3 = (bf16[2,2064,128]{2,1,0:T(8,128)(2,1)}, bf16[2,2064,128]{2,1,0:T(8,128)(2,1)S(1)}, u32[]{:S(2)}, u32[]{:S(2)}) collective-permute-start(bf16[2,2064,128]{2,1,0:T(8,128)(2,1)} %refs_0_.4), channel_id=1, source_target_pairs={{0,4},{4,0},{8,12},{12,8},{1,5},{5,1},{9,13},{13,9},{2,6},{6,2},{1... | collective-permute-start | bytes 3170312 | tf_op jit(solution)/shard_map/ppermute | solution.py:33
  1.2 8.8 %collective-permute-start.1 = (bf16[192,2,2,128]{3,2,1,0:T(2,128)(2,1)}, bf16[192,2,2,128]{3,2,1,0:T(2,128)(2,1)S(1)}, u32[]{:S(2)}, u32[]{:S(2)}) collective-permute-start(bf16[192,2,2,128]{3,2,1,0:T(2,128)(2,1)} %refs_0_.3), channel_id=1, source_target_pairs={{0,8},{4,12},{8,0},{12,4},{1,9},{5,13},{9,1},{13,5},{2,10},{6,14},... | collective-permute-start | bytes 589832 | tf_op jit(solution)/shard_map/ppermute | solution.py:33
  6.3 3.1 %copy-start.2 = (bf16[192,2,2,128]{3,2,1,0:T(2,128)(2,1)S(1)}, bf16[192,2,2,128]{3,2,1,0:T(2,128)(2,1)}, u32[]{:S(2)}) copy-start(bf16[192,2,2,128]{3,2,1,0:T(2,128)(2,1)} %refs_0_.3) | copy-start | bytes 589828
  6.4 6.1 %copy-start = (bf16[2,2064,128]{2,1,0:T(8,128)(2,1)S(1)}, bf16[2,2064,128]{2,1,0:T(8,128)(2,1)}, u32[]{:S(2)}) copy-start(bf16[2,2064,128]{2,1,0:T(8,128)(2,1)} %refs_0_.4) | copy-start | bytes 3170308
  9.3 3.3 %copy-start.1 = (bf16[192,2,5,128]{3,1,2,0:T(2,128)(2,1)S(1)}, bf16[192,2,5,128]{3,1,2,0:T(2,128)(2,1)}, u32[]{:S(2)}) copy-start(bf16[192,2,5,128]{3,1,2,0:T(2,128)(2,1)} %param.7) | copy-start | bytes 1474564
  9.3 1.8 %collective-permute-start.4 = (bf16[32,7,2,128]{3,2,1,0:T(2,128)(2,1)S(1)}, bf16[32,7,2,128]{3,2,1,0:T(2,128)(2,1)S(1)}, u32[]{:S(2)}, u32[]{:S(2)}) collective-permute-start(bf16[32,7,2,128]{3,2,1,0:T(2,128)(2,1)S(1)} %shard_map.94), channel_id=1, source_target_pairs={{0,4},{4,0},{8,12},{12,8},{1,5},{5,1},{9,13},{13,9},{2,6},{6,2},{1... | collective-permute-start | bytes 344072 | tf_op jit(solution)/shard_map/ppermute | solution.py:33
  9.4 3.1 %collective-permute-start = (bf16[192,2,2,128]{3,2,1,0:T(2,128)(2,1)S(1)}, bf16[192,2,2,128]{3,2,1,0:T(2,128)(2,1)S(1)}, u32[]{:S(2)}, u32[]{:S(2)}) collective-permute-start(bf16[192,2,2,128]{3,2,1,0:T(2,128)(2,1)S(1)} %copy-done.2), channel_id=1, source_target_pairs={{0,4},{4,0},{8,12},{12,8},{1,5},{5,1},{9,13},{13,9},{2,6},{6,2},{1... | collective-permute-start | bytes 589832 | tf_op jit(solution)/shard_map/ppermute | solution.py:33
  9.9 14.8 %collective-permute-start.7 = (bf16[2064,128]{1,0:T(8,128)(2,1)}, bf16[2064,128]{1,0:T(8,128)(2,1)S(1)}, u32[]{:S(2)}, u32[]{:S(2)}) collective-permute-start(bf16[2064,128]{1,0:T(8,128)(2,1)} %slice_bitcast_fusion.1), channel_id=1, source_target_pairs={{0,8},{4,12},{8,0},{12,4},{1,9},{5,13},{9,1},{13,5},{2,10},{6,14},... | collective-permute-start | bytes 1585160 | tf_op jit(solution)/shard_map/ppermute | solution.py:33
  11.2 1.4 %collective-permute-start.2 = (bf16[192,2,2,128]{3,2,1,0:T(2,128)(2,1)S(1)}, bf16[192,2,2,128]{3,2,1,0:T(2,128)(2,1)S(1)}, u32[]{:S(2)}, u32[]{:S(2)}) collective-permute-start(bf16[192,2,2,128]{3,2,1,0:T(2,128)(2,1)S(1)} %collective-permute-done.1.refs_2_), channel_id=1, source_target_pairs={{0,4},{4,0},{8,12},{12,8},{1,5},{5,1},{9,13},{13,9},{2,6},{6,2},{1... | collective-permute-start | bytes 589832 | tf_op jit(solution)/shard_map/ppermute | solution.py:33
  11.6 13.7 %collective-permute-start.5 = (bf16[104,2,128]{2,1,0:T(2,128)(2,1)S(1)}, bf16[104,2,128]{2,1,0:T(2,128)(2,1)S(1)}, u32[]{:S(2)}, u32[]{:S(2)}) collective-permute-start(bf16[104,2,128]{2,1,0:T(2,128)(2,1)S(1)} %get-tuple-element.54), channel_id=1, source_target_pairs={{0,8},{4,12},{8,0},{12,4},{1,9},{5,13},{9,1},{13,5},{2,10},{6,14},... | collective-permute-start | bytes 159752 | tf_op jit(solution)/shard_map/ppermute | solution.py:33
  25.3 7.9 %collective-permute-start.8 = (bf16[2064,128]{1,0:T(8,128)(2,1)S(1)}, bf16[2064,128]{1,0:T(8,128)(2,1)S(1)}, u32[]{:S(2)}, u32[]{:S(2)}) collective-permute-start(bf16[2064,128]{1,0:T(8,128)(2,1)S(1)} %collective-permute-done.7.refs_2_), channel_id=1, source_target_pairs={{0,4},{4,0},{8,12},{12,8},{1,5},{5,1},{9,13},{13,9},{2,6},{6,2},{1... | collective-permute-start | bytes 1585160 | tf_op jit(solution)/shard_map/ppermute | solution.py:33
  25.3 14.4 %collective-permute-start.6 = (bf16[2064,128]{1,0:T(8,128)(2,1)S(1)}, bf16[2064,128]{1,0:T(8,128)(2,1)S(1)}, u32[]{:S(2)}, u32[]{:S(2)}) collective-permute-start(bf16[2064,128]{1,0:T(8,128)(2,1)S(1)} %slice_bitcast_fusion), channel_id=1, source_target_pairs={{0,8},{4,12},{8,0},{12,4},{1,9},{5,13},{9,1},{13,5},{2,10},{6,14},... | collective-permute-start | bytes 1585160 | tf_op jit(solution)/shard_map/ppermute | solution.py:33
  39.7 1.9 %collective-permute-start.9 = (bf16[2064,128]{1,0:T(8,128)(2,1)S(1)}, bf16[2064,128]{1,0:T(8,128)(2,1)S(1)}, u32[]{:S(2)}, u32[]{:S(2)}) collective-permute-start(bf16[2064,128]{1,0:T(8,128)(2,1)S(1)} %collective-permute-done.6.refs_0_), channel_id=1, source_target_pairs={{0,4},{4,0},{8,12},{12,8},{1,5},{5,1},{9,13},{13,9},{2,6},{6,2},{1... | collective-permute-start | bytes 1585160 | tf_op jit(solution)/shard_map/ppermute | solution.py:33
